TPU v7x, 32 devices: a whole 2x2x4 slice. The times are simulated.
32 devices in a mesh: dp: 8 (over z, x), expert: 4 (over y, core).
Axes of the slice: x: 2, y: 2, z: 4, core: 2. Of those that a mesh axis runs over, the one named last changes fastest.
Arguments:
- out_grad: bfloat16 [512, 3072], P('expert'), may hold values from -1.1953125 to 1.1953125
- routes: int32 [512, 4], P('expert'), may hold values from 0 to 7, all different within a row; in each aligned block of 128 rows (0 to 127, 128 to 255, ...) at most 80 rows name the same one
- gate_values: float32 [512, 4], P('expert'), may hold values from 0.1 to 0.5
- layer_input: bfloat16 [512, 3072], P('expert'), may hold values from -6 to 6
- w_gate: bfloat16 [8, 3072, 8192], P('expert', None, 'dp'), may hold values from -0.109375 to 0.109375
- w_up: bfloat16 [8, 3072, 8192], P('expert', None, 'dp'), may hold values from -0.109375 to 0.109375
- w_down: bfloat16 [8, 3072, 8192], P('expert', None, 'dp'), may hold values from -0.109375 to 0.109375
Outputs:
- input_grad: bfloat16 [512, 3072], P('expert')
- grad_gate: float32 [8, 3072, 8192], P('expert', None, 'dp')
- grad_up: float32 [8, 3072, 8192], P('expert', None, 'dp')
Inputs may be any that keep to these rules, and one draw needn't show every extreme that they name: In every aligned block of 128 tokens (the tokens of one index of expert) no expert is named by more than 80 routes, a bound that some block reaches; the 4 experts of a token differ.
All inputs are finite; a program needn't handle non-finite values.
Results may differ from a plain program's by a relative error of at most 0.024.
Values may be sent and summed in bfloat16 or wider, within the bound.
No kernel may reach another device: no remote copies, remote signals or barrier semaphores. Data moves between devices by JAX's collectives and lax.ppermute only.
A program may use at most 192 MiB of HBM per device.

v0:
```python
import functools

import jax
import jax.numpy as jnp
from jax import lax
from jax.experimental import pallas as pl
from jax.experimental.pallas import tpu as pltpu
from jax.sharding import PartitionSpec as P

EXPERTS = 8
MOST = 80
UNIT_TILE = 512
FEATURE_TILE = 512
BF16 = jnp.bfloat16
F32 = jnp.float32
NN = (((1,), (0,)), ((), ()))
NT = (((1,), (1,)), ((), ()))
TN = (((0,), (0,)), ((), ()))


def dot(a, b, dims=NN):
    return lax.dot_general(a, b, dims, preferred_element_type=F32)


def params(count, mebibytes):
    return pltpu.CompilerParams(
        dimension_semantics=("arbitrary",) * count, vmem_limit_bytes=mebibytes * 1024 * 1024
    )


def whole(shape):
    return pl.BlockSpec(
        shape, lambda *_: (0,) * len(shape), pipeline_mode=pl.Buffered(buffer_count=1)
    )


def one_hot(slot_row):
    slots = lax.broadcasted_iota(jnp.int32, (MOST, slot_row.shape[1]), 0)
    return slots == slot_row.astype(jnp.int32)


def lay_out(held, pieces, first):
    rows, at = held.shape[0], 0
    for piece in pieces:
        low, high = max(first, at), min(first + rows, at + piece.shape[0])
        if low < high:
            held[low - first : high - first] = piece[low - at : high - at]
        at += piece.shape[0]


def column_chunks(features):
    step = 768 if features % 768 == 0 else features
    return [slice(c, c + step) for c in range(0, features, step)]


def dispatch(pieces, slot, held, chosen, out, weight=None):
    experts, blocks, tokens = slot.shape
    group = held.shape[0] // tokens
    places = [(l, b) for l in range(experts) for b in range(group)]
    for start in range(0, blocks, group):
        chosen[...] = jnp.zeros_like(chosen)
        scales = []
        for i, (l, b) in enumerate(places):
            at = slice(start + b, start + b + 1)
            mask = one_hot(slot[l, at, :])
            chosen[i * MOST : (i + 1) * MOST, b * tokens : (b + 1) * tokens] = mask.astype(BF16)
            if weight is not None:
                scales.append(
                    jnp.sum(jnp.where(mask, weight[l, at, :], 0.0), axis=1, keepdims=True)
                )
        lay_out(held, pieces, start * tokens)
        for cols in column_chunks(held.shape[1]):
            taken = dot(chosen[...], held[:, cols])
            for i, (l, b) in enumerate(places):
                part = taken[i * MOST : (i + 1) * MOST]
                if scales:
                    part = part * scales[i]
                span = slice((start + b) * MOST, (start + b + 1) * MOST)
                out[l, span, cols] = part.astype(BF16)


def dispatch_scratch(experts, blocks, tokens, features):
    group = 2 if blocks % 2 == 0 else 1
    return [
        pltpu.VMEM((group * tokens, features), BF16),
        pltpu.VMEM((experts * group * MOST, group * tokens), BF16),
        pltpu.VMEM((experts, blocks * MOST, features), BF16),
    ]


def forward_kernel(count, *refs):
    pieces, (slot, w_gate, w_up, rows_out, act, slope) = refs[:count], refs[count : count + 6]
    held, chosen, rows, sent = refs[count + 6 :]
    expert, tile = pl.program_id(0), pl.program_id(1)
    copy = pltpu.make_async_copy(rows, rows_out, sent)

    @pl.when((expert == 0) & (tile == 0))
    def _():
        dispatch(pieces, slot, held, chosen, rows)
        copy.start()

    x = rows[expert]
    gate = dot(x, w_gate[0])
    up = dot(x, w_up[0])
    sig = jax.nn.sigmoid(gate)
    act[0] = gate * sig
    slope[0] = up * sig * (1.0 + gate * (1.0 - sig))

    @pl.when((expert == pl.num_programs(0) - 1) & (tile == pl.num_programs(1) - 1))
    def _():
        copy.wait()


def forward(pieces, slot, w_gate, w_up):
    experts, blocks, tokens = slot.shape
    _, features, units = w_gate.shape
    tile = min(UNIT_TILE, units)
    slots = blocks * MOST
    matrix = pl.BlockSpec((1, features, tile), lambda l, f: (l, 0, f))
    unit = pl.BlockSpec((1, slots, tile), lambda l, f: (l, 0, f))
    return pl.pallas_call(
        functools.partial(forward_kernel, len(pieces)),
        grid=(experts, units // tile),
        in_specs=[whole(p.shape) for p in pieces] + [whole(slot.shape), matrix, matrix],
        out_specs=[pl.BlockSpec(memory_space=pltpu.HBM), unit, unit],
        out_shape=[
            jax.ShapeDtypeStruct((experts, slots, features), BF16),
            jax.ShapeDtypeStruct((experts, slots, units), F32),
            jax.ShapeDtypeStruct((experts, slots, units), F32),
        ],
        scratch_shapes=dispatch_scratch(experts, blocks, tokens, features)
        + [pltpu.SemaphoreType.DMA],
        compiler_params=params(2, 52),
        cost_estimate=pl.CostEstimate(
            flops=4 * experts * slots * features * units,
            bytes_accessed=4 * experts * features * units,
            transcendentals=experts * slots * units,
        ),
    )(*pieces, slot, w_gate, w_up)


def hidden_kernel(count, *refs):
    pieces, (slot, weight, act, slope, w_down) = refs[:count], refs[count : count + 5]
    gate_grad, up_grad, held, chosen, grads = refs[count + 5 :]
    expert = pl.program_id(0)

    @pl.when((expert == 0) & (pl.program_id(1) == 0))
    def _():
        dispatch(pieces, slot, held, chosen, grads, weight)

    hidden = dot(grads[expert], w_down[0])
    up_grad[0] = (hidden * act[0]).astype(BF16)
    gate_grad[0] = (hidden * slope[0]).astype(BF16)


def hidden_grads(pieces, slot, weight, act, slope, w_down):
    experts, blocks, tokens = slot.shape
    _, features, units = w_down.shape
    tile = min(UNIT_TILE, units)
    slots = blocks * MOST
    unit = pl.BlockSpec((1, slots, tile), lambda l, f: (l, 0, f))
    return pl.pallas_call(
        functools.partial(hidden_kernel, len(pieces)),
        grid=(experts, units // tile),
        in_specs=[whole(p.shape) for p in pieces]
        + [whole(slot.shape), whole(slot.shape), unit, unit]
        + [pl.BlockSpec((1, features, tile), lambda l, f: (l, 0, f))],
        out_specs=[unit, unit],
        out_shape=[jax.ShapeDtypeStruct((experts, slots, units), BF16)] * 2,
        scratch_shapes=dispatch_scratch(experts, blocks, tokens, features),
        compiler_params=params(2, 48),
        cost_estimate=pl.CostEstimate(
            flops=2 * experts * slots * features * units,
            bytes_accessed=2 * experts * features * units,
            transcendentals=0,
        ),
    )(*pieces, slot, weight, act, slope, w_down)


def inputs_kernel(groups, back, gate_grad, up_grad, w_gate, w_up, *refs):
    sums, held = refs[:-1], refs[-1]
    blocks, tokens, _ = back.shape
    for l in range(gate_grad.shape[0]):
        partial = dot(gate_grad[l], w_gate[l], NT) + dot(up_grad[l], w_up[l], NT)
        for b in range(blocks):
            held[b, l * MOST : (l + 1) * MOST] = partial[b * MOST : (b + 1) * MOST].astype(BF16)
    for out, members in zip(sums, groups):
        for place, b in enumerate(members):
            out[place * tokens : (place + 1) * tokens] = dot(back[b], held[b]).astype(BF16)


def input_sums(back, gate_grad, up_grad, w_gate, w_up, groups, part, parts):
    blocks, tokens, _ = back.shape
    experts, features, units = w_gate.shape
    wide = FEATURE_TILE
    steps = features // parts // wide
    slots = blocks * MOST
    across = pl.BlockSpec((experts, wide, units), lambda i: (0, part * steps + i, 0))
    return pl.pallas_call(
        functools.partial(inputs_kernel, groups),
        grid=(steps,),
        in_specs=[whole(back.shape), whole(gate_grad.shape), whole(up_grad.shape), across, across],
        out_specs=[pl.BlockSpec((len(g) * tokens, wide), lambda i: (0, i)) for g in groups],
        out_shape=[
            jax.ShapeDtypeStruct((len(g) * tokens, features // parts), BF16) for g in groups
        ],
        scratch_shapes=[pltpu.VMEM((blocks, experts * MOST, wide), BF16)],
        compiler_params=params(1, 40),
        cost_estimate=pl.CostEstimate(
            flops=4 * experts * slots * features * units // parts,
            bytes_accessed=4 * experts * features * units // parts,
            transcendentals=0,
        ),
    )(back, gate_grad, up_grad, w_gate, w_up)


def back_matrix(slot):
    places = jnp.arange(MOST, dtype=F32)
    slot = lax.optimization_barrier(slot.transpose(1, 2, 0))
    parts = [slot[..., l : l + 1] == places for l in range(slot.shape[2])]
    return jnp.concatenate([p.astype(BF16) for p in parts], axis=2)


def weights_kernel(rows, gate_grad, up_grad, *refs):
    grad_gate, grad_up = refs[-2:]
    grad_gate[0] = dot(rows[0], gate_grad[0], TN)
    grad_up[0] = dot(rows[0], up_grad[0], TN)


def weight_grads(rows, gate_grad, up_grad, before, expert, first=0, steps=None):
    experts, slots, features = rows.shape
    units = gate_grad.shape[2]
    wide = FEATURE_TILE
    steps = features // wide if steps is None else steps
    unit = pl.BlockSpec((1, slots, units), lambda d: (expert, 0, 0))
    out = pl.BlockSpec((1, wide, units), lambda d: (expert, first + d, 0))
    kept = [] if before is None else list(before)
    return pl.pallas_call(
        weights_kernel,
        grid=(steps,),
        in_specs=[
            pl.BlockSpec((1, slots, wide), lambda d: (expert, 0, first + d)), unit, unit
        ]
        + [pl.BlockSpec(memory_space=pl.ANY)] * len(kept),
        out_specs=[out, out],
        out_shape=[jax.ShapeDtypeStruct((experts, features, units), F32)] * 2,
        input_output_aliases={3 + i: i for i in range(len(kept))},
        compiler_params=params(1, 30),
        cost_estimate=pl.CostEstimate(
            flops=4 * slots * steps * wide * units,
            bytes_accessed=8 * steps * wide * units,
            transcendentals=0,
        ),
    )(rows, gate_grad, up_grad, *kept)


def route_table(routes, gate_values):
    tokens = routes.shape[0]
    experts = jnp.arange(EXPERTS, dtype=jnp.int32)[:, None, None]
    match = routes.T[None] == experts
    member = jnp.any(match, axis=1)
    gate = jnp.sum(jnp.where(match, gate_values.T[None], 0.0), axis=1)
    place = jnp.arange(tokens, dtype=jnp.int32)
    earlier = (place[:, None] < place[None, :]).astype(BF16)
    slot = jnp.where(member, dot(member.astype(BF16), earlier), -1.0)
    return jnp.stack([slot, gate], axis=1)


def flip(value, axis, bit):
    count = lax.axis_size(axis)
    return lax.ppermute(value, axis, [(i, i ^ bit) for i in range(count)])


def swap_order(value, side, pair, dim):
    shape = value.shape
    value = value.reshape(shape[:dim] + (2, 2, shape[dim] // 4) + shape[dim + 1 :])
    value = jnp.where(side == 1, jnp.flip(value, dim), value)
    return jnp.where(pair == 1, jnp.flip(value, dim + 1), value).reshape(shape)


def add(*terms):
    total = terms[0].astype(F32)
    for term in terms[1:]:
        total = total + term.astype(F32)
    return total.astype(BF16)


def quarters(value, count, at):
    return lax.dynamic_slice_in_dim(value, at * (count // 4), count // 4, 0)


def local_near(out_grad, routes, gate_values, layer_input, w_gate, w_up, w_down):
    experts, features, _ = w_gate.shape
    me = lax.axis_index("expert")
    position = lax.axis_index("dp")
    side, pair = position % 2, position // 2 % 2
    tokens = out_grad.shape[0]
    half, quarter = tokens // 2, tokens // 4
    corner = side * 2 + pair

    def to_core(values):
        return tuple(flip(v, "expert", 1) for v in values)

    x_mine = jnp.concatenate(
        [quarters(layer_input, tokens, q) for q in (corner, 3 - corner)], axis=0
    )
    x_mine, layer_input, out_grad, routes = lax.optimization_barrier(
        (x_mine, layer_input, out_grad, routes)
    )
    x_across = flip(x_mine, "expert", 2)
    x_sibling, g_sibling = to_core((layer_input, out_grad))
    x_sibling, routes = lax.optimization_barrier((x_sibling, routes))
    table = route_table(routes, gate_values)
    tables = []
    for r in range(4):
        part = lax.dynamic_slice_in_dim(table, (me ^ r) * experts, experts, 0)
        tables.append(flip(part, "expert", r) if r > 0 else part)
    x_across, g_own = lax.optimization_barrier((x_across, out_grad))
    x_far = (x_across, flip(x_across[:quarter], "dp", 1), flip(x_across[:quarter], "dp", 2))
    g_across = flip(g_own, "expert", 2)
    x_far = (*x_far, *to_core(x_far))
    table = jnp.stack(tables, axis=2)
    slot, weight = table[:, 0], table[:, 1]
    back = back_matrix(swap_order(slot, side, pair, 2))
    far = swap_order(slot[:, 2:], side, pair, 2).reshape(experts, 2, 4, quarter)
    far = jnp.stack([far[:, :, q] for q in (0, 3, 2, 1)], axis=2).reshape(experts, 2, tokens)
    slot_x = jnp.concatenate([slot[:, :2], far], axis=1)
    slot_x, back = lax.optimization_barrier((slot_x, back))
    rows, act, slope = forward((layer_input, x_sibling, *x_far), slot_x, w_gate, w_up)
    act, g_across = lax.optimization_barrier((act, g_across))
    gate_grad, up_grad = hidden_grads(
        (out_grad, g_sibling, g_across, *to_core((g_across,))), slot, weight, act, slope, w_down
    )

    groups = ((0, 2), (1, 3))
    kept_a, sent_a = input_sums(back, gate_grad, up_grad, w_gate, w_up, groups, 0, 2)
    kept_b, sent_b = input_sums(back, gate_grad, up_grad, w_gate, w_up, groups, 1, 2)

    def piece(after, before, *which):
        held, rows_now = lax.optimization_barrier((after, rows))
        return held, weight_grads(rows_now, gate_grad, up_grad, before, *which)

    def corners(value):
        return [flip(v, "dp", step) for v, step in zip(value, (2, 1, 3))]

    def cut(value, count):
        return [value[i : i + quarter] for i in range(0, count * quarter, quarter)]

    chip_a = add(kept_a, flip(sent_a, "expert", 1))
    got = flip(sent_b, "expert", 1)
    chip_b = [add(a, b) for a, b in zip(cut(kept_b, 8), cut(got, 8))]
    far_a = chip_a[tokens:]
    away = [jnp.concatenate([chip_b[q], chip_b[4 + q]], axis=0) for q in (1, 2, 3)]
    (far_a, *away), grads = piece((far_a, *away), None, 0, 0, 5)
    got_a, got_b = flip(far_a, "expert", 2), corners(away)
    got_a, got_b, *grads = lax.optimization_barrier((got_a, got_b, *grads))
    own_a = [add(a, b) for a, b in zip(cut(chip_a, 4), cut(got_a, 4))]
    mine_b = add(chip_b[0], *(v[:quarter] for v in got_b))
    far_b = add(chip_b[4], *(v[quarter:] for v in got_b))
    (far_b, *own_a), grads = piece((far_b, *own_a), grads, 0, 5, 1)
    got_a, got_b = corners(own_a[1:]), flip(far_b, "expert", 2)
    got_a, got_b, *grads = lax.optimization_barrier((got_a, got_b, *grads))
    mine = jnp.concatenate([add(own_a[0], *got_a), add(mine_b, got_b)], axis=1)
    mine, grads = piece(mine, grads, 1, 0, 3)
    got = flip(mine, "dp", 4)
    got, *grads = lax.optimization_barrier((got, *grads))
    mine = add(mine, got)
    mine, grads = piece(mine, grads, 1, 3, 3)
    got = corners([mine] * 3)
    got, *grads = lax.optimization_barrier((got, *grads))
    total = swap_order(jnp.concatenate([mine, *got], axis=0), side, pair, 0)
    return (total, *grads)


def local_any(out_grad, routes, gate_values, layer_input, w_gate, w_up, w_down):
    experts = w_gate.shape[0]
    me = lax.axis_index("expert")
    rows_in = lax.all_gather(layer_input, "expert", tiled=True)
    grads_in = lax.all_gather(out_grad, "expert", tiled=True)
    table = lax.all_gather(route_table(routes, gate_values), "expert")
    table = lax.dynamic_slice_in_dim(table, me * experts, experts, 1).transpose(1, 2, 0, 3)
    slot, weight = table[:, 0], table[:, 1]
    rows, act, slope = forward([rows_in], slot, w_gate, w_up)
    gate_grad, up_grad = hidden_grads([grads_in], slot, weight, act, slope, w_down)
    groups = (tuple(range(slot.shape[1])),)
    (sums,) = input_sums(back_matrix(slot), gate_grad, up_grad, w_gate, w_up, groups, 0, 1)
    grads = None
    for l in range(experts):
        grads = weight_grads(rows, gate_grad, up_grad, grads, l)
    own = lax.psum_scatter(sums, "expert", scatter_dimension=0, tiled=True)
    return (lax.psum(own, "dp"), *grads)


def solution(mesh):
    near = mesh.shape["dp"] == 8 and mesh.shape["expert"] == 4
    placed = (
        P("expert", None),
        P("expert", None),
        P("expert", None),
        P("expert", None),
        P("expert", None, "dp"),
        P("expert", None, "dp"),
        P("expert", None, "dp"),
    )
    return jax.shard_map(
        local_near if near else local_any,
        mesh=mesh,
        in_specs=placed,
        out_specs=(P("expert", None), P("expert", None, "dp"), P("expert", None, "dp")),
        check_vma=False,
    )
```

profile of v0, /device:TPU:0, one launch (start us, length us, event | category | flops | bytes accessed | tf_op | source)
XLA Modules:
  0.0 118.0 jit_solution(907783769826007121)
XLA Ops:
  0.7 1.1 constant_dynamic-slice_fusion.1
  1.8 0.5 collective-permute-start
  2.3 2.6 %collective-permute-start.5 = (bf16[64,3072]{1,0:T(8,128)(2,1)S(1)}, bf16[64,3072]{1,0:T(8,128)(2,1)S(1)}, u32[]{:S(2)}, u32[]{:S(2)}) collective-permute-start(bf16[64,3072]{1,0:T(8,128)(2,1)S(1)} %pad_maximum_fusion.1), channel_id=1, source_target_pairs={{0,2},{1,3},{2,0},{3,1},{4,6},{5,7},{6,4},{7,5},{8,10},{9,11},{10,... | collective-permute-start | bytes 1179656 | tf_op jit(solution)/shard_map/ppermute | solution.py:271
  4.9 9.7 %collective-permute-done.5.refs_2_ = bf16[64,3072]{1,0:T(8,128)(2,1)S(1)} collective-permute-done((bf16[64,3072]{1,0:T(8,128)(2,1)S(1)}, bf16[64,3072]{1,0:T(8,128)(2,1)S(1)}, u32[]{:S(2)}, u32[]{:S(2)}) %collective-permute-start.5) | collective-permute-done | bytes 393248 | tf_op jit(solution)/shard_map/ppermute | solution.py:271
  14.6 1.9 %collective-permute-start.7 = (bf16[32,3072]{1,0:T(8,128)(2,1)S(1)}, bf16[32,3072]{1,0:T(8,128)(2,1)S(1)}, u32[]{:S(2)}, u32[]{:S(2)}) collective-permute-start(bf16[32,3072]{1,0:T(8,128)(2,1)S(1)} %slice.136), channel_id=1, source_target_pairs={{0,8},{4,12},{8,0},{12,4},{16,24},{20,28},{24,16},{28,20},{1,9},{5... | collective-permute-start | bytes 589832 | tf_op jit(solution)/shard_map/ppermute | solution.py:271
  16.5 1.5 %collective-permute-start.6 = (bf16[32,3072]{1,0:T(8,128)(2,1)S(1)}, bf16[32,3072]{1,0:T(8,128)(2,1)S(1)}, u32[]{:S(2)}, u32[]{:S(2)}) collective-permute-start(bf16[32,3072]{1,0:T(8,128)(2,1)S(1)} %slice.136), channel_id=1, source_target_pairs={{0,4},{4,0},{8,12},{12,8},{16,20},{20,16},{24,28},{28,24},{1,5},{5... | collective-permute-start | bytes 589832 | tf_op jit(solution)/shard_map/ppermute | solution.py:271
  18.0 0.7 fusion.1
  18.8 0.7 select_reduce_fusion
  19.6 1.6 %collective-permute-start.2 = (f32[2,2,128]{2,0,1:T(2,128)S(1)}, f32[2,2,128]{2,0,1:T(2,128)S(1)}, u32[]{:S(2)}, u32[]{:S(2)}) collective-permute-start(f32[2,2,128]{2,0,1:T(2,128)S(1)} %get-tuple-element.152), channel_id=1, source_target_pairs={{0,2},{1,3},{2,0},{3,1},{4,6},{5,7},{6,4},{7,5},{8,10},{9,11},{10,... | collective-permute-start | bytes 6152 | tf_op jit(solution)/shard_map/ppermute | solution.py:271
  21.2 0.3 collective-permute-start.3
  21.5 0.3 collective-permute-start.4
  21.8 0.8 collective-permute-done.6.refs_3_
  22.7 1.5 %collective-permute-start.11 = (bf16[128,3072]{1,0:T(8,128)(2,1)}, bf16[128,3072]{1,0:T(8,128)(2,1)S(1)}, u32[]{:S(2)}, u32[]{:S(2)}) collective-permute-start(bf16[128,3072]{1,0:T(8,128)(2,1)} %refs_0_.1), channel_id=1, source_target_pairs={{0,2},{1,3},{2,0},{3,1},{4,6},{5,7},{6,4},{7,5},{8,10},{9,11},{10,... | collective-permute-start | bytes 2359304 | tf_op jit(solution)/shard_map/ppermute | solution.py:271
  24.2 0.2 collective-permute-start.10
  24.4 0.3 collective-permute-start.9
  25.3 0.2 iota_compare_fusion
  25.5 0.2 add_convert_fusion.1.back
  25.9 15.9 %shard_map.94 = (bf16[2,320,3072]{2,1,0:T(8,128)(2,1)}, f32[2,320,1024]{2,1,0:T(8,128)}, f32[2,320,1024]{2,1,0:T(8,128)}) custom-call(bf16[128,3072]{1,0:T(8,128)(2,1)} %refs_0_, bf16[128,3072]{1,0:T(8,128)(2,1)} %copy-done.2, bf16[64,3072]{1,0:T(8,128)(2,1)S(1)} %collective-permute-done.5.refs_2_, bf16[32,3072]{1,0:T(8,128)(2,1)S(1)} %collective-permute-done.6.refs_3_, ...), custom_call_target="tpu_custom_call" | custom-call | flops 8053063680 | bytes 25165824 | tf_op jit(solution)/shard_map/pallas_call | solution.py:121
  41.9 1.0 collective-permute-done.11.refs_2_
  42.9 2.3 %collective-permute-done.12.refs_3_ = bf16[128,3072]{1,0:T(8,128)(2,1)S(1)} collective-permute-done((bf16[128,3072]{1,0:T(8,128)(2,1)S(1)}, bf16[128,3072]{1,0:T(8,128)(2,1)S(1)}, u32[]{:S(2)}, u32[]{:S(2)}) %collective-permute-start.12) | collective-permute-done | bytes 786464 | tf_op jit(solution)/shard_map/ppermute | solution.py:271
  45.1 9.9 %shard_map.95 = (bf16[2,320,1024]{2,1,0:T(8,128)(2,1)S(1)}, bf16[2,320,1024]{2,1,0:T(8,128)(2,1)S(1)}) custom-call(bf16[128,3072]{1,0:T(8,128)(2,1)S(1)} %copy-done.1, bf16[128,3072]{1,0:T(8,128)(2,1)S(1)} %collective-permute-done.4.refs_1_, bf16[128,3072]{1,0:T(8,128)(2,1)S(1)} %collective-permute-done.11.refs_2_, ...), custom_call_target="tpu_custom_call" | custom-call | flops 4026531840 | bytes 12582912 | tf_op jit(solution)/shard_map/pallas_call | solution.py:162
  55.0 8.1 %shard_map.97 = (bf16[256,1536]{1,0:T(8,128)(2,1)S(1)}, bf16[256,1536]{1,0:T(8,128)(2,1)S(1)}) custom-call(bf16[4,128,160]{2,1,0:T(8,128)(2,1)S(1)} %add_convert_fusion.1.back, bf16[2,320,1024]{2,1,0:T(8,128)(2,1)S(1)} %get-tuple-element.81.gate_grad, bf16[2,320,1024]{2,1,0:T(8,128)(2,1)S(1)} %get-tuple-element.82.up_grad, bf16[2,3072,1024]{2,1,0:T(8,128)(2,1)} %w_gate.3, ...), custom_call_target="tpu_custom_call" | custom-call | flops 4026531840 | bytes 12582912 | tf_op jit(solution)/shard_map/pallas_call | solution.py:199
  63.1 0.2 collective-permute-start.14
  63.3 8.1 %shard_map.96 = (bf16[256,1536]{1,0:T(8,128)(2,1)S(1)}, bf16[256,1536]{1,0:T(8,128)(2,1)S(1)}) custom-call(bf16[4,128,160]{2,1,0:T(8,128)(2,1)S(1)} %add_convert_fusion.1.back, bf16[2,320,1024]{2,1,0:T(8,128)(2,1)S(1)} %get-tuple-element.81.gate_grad, bf16[2,320,1024]{2,1,0:T(8,128)(2,1)S(1)} %get-tuple-element.82.up_grad, bf16[2,3072,1024]{2,1,0:T(8,128)(2,1)} %w_gate.3, ...), custom_call_target="tpu_custom_call" | custom-call | flops 4026531840 | bytes 12582912 | tf_op jit(solution)/shard_map/pallas_call | solution.py:199
  71.5 0.4 collective-permute-start.13
  72.1 1.7 %collective-permute-done.13 = bf16[256,1536]{1,0:T(8,128)(2,1)S(1)} collective-permute-done((bf16[256,1536]{1,0:T(8,128)(2,1)S(1)}, bf16[256,1536]{1,0:T(8,128)(2,1)S(1)}, u32[]{:S(2)}, u32[]{:S(2)}) %collective-permute-start.13) | collective-permute-done | bytes 786464 | tf_op jit(solution)/shard_map/ppermute | solution.py:271
  74.0 1.6 %collective-permute-start.15 = (bf16[128,1536]{1,0:T(8,128)(2,1)S(1)}, bf16[128,1536]{1,0:T(8,128)(2,1)S(1)}, u32[]{:S(2)}, u32[]{:S(2)}) collective-permute-start(bf16[128,1536]{1,0:T(8,128)(2,1)S(1)} %slice.180), channel_id=1, source_target_pairs={{0,2},{1,3},{2,0},{3,1},{4,6},{5,7},{6,4},{7,5},{8,10},{9,11},{10,... | collective-permute-start | bytes 1179656 | tf_op jit(solution)/shard_map/ppermute | solution.py:271
  75.6 0.4 collective-permute-start.16
  76.1 1.5 %collective-permute-start.17 = (bf16[64,1536]{1,0:T(8,128)(2,1)S(1)}, bf16[64,1536]{1,0:T(8,128)(2,1)S(1)}, u32[]{:S(2)}, u32[]{:S(2)}) collective-permute-start(bf16[64,1536]{1,0:T(8,128)(2,1)S(1)} %pad_maximum_fusion.3), channel_id=1, source_target_pairs={{0,4},{4,0},{8,12},{12,8},{16,20},{20,16},{24,28},{28,24},{1,5},{5... | collective-permute-start | bytes 589832 | tf_op jit(solution)/shard_map/ppermute | solution.py:271
  77.6 1.5 %collective-permute-start.18 = (bf16[64,1536]{1,0:T(8,128)(2,1)S(1)}, bf16[64,1536]{1,0:T(8,128)(2,1)S(1)}, u32[]{:S(2)}, u32[]{:S(2)}) collective-permute-start(bf16[64,1536]{1,0:T(8,128)(2,1)S(1)} %pad_maximum_fusion.4), channel_id=1, source_target_pairs={{0,12},{4,8},{8,4},{12,0},{16,28},{20,24},{24,20},{28,16},{1,13},{... | collective-permute-start | bytes 589832 | tf_op jit(solution)/shard_map/ppermute | solution.py:271
  79.1 8.2 %shard_map.98 = (f32[2,3072,1024]{2,1,0:T(8,128)}, f32[2,3072,1024]{2,1,0:T(8,128)}) custom-call(bf16[2,320,3072]{2,1,0:T(8,128)(2,1)S(1)} %copy-done, bf16[2,320,1024]{2,1,0:T(8,128)(2,1)S(1)} %get-tuple-element.81.gate_grad, bf16[2,320,1024]{2,1,0:T(8,128)(2,1)S(1)} %get-tuple-element.82.up_grad), custom_call_target="tpu_custom_call" | custom-call | flops 3355443200 | bytes 20971520 | tf_op jit(solution)/shard_map/pallas_call | solution.py:238
  87.3 0.3 collective-permute-done.18
  87.8 0.9 collective-permute-start.19
  88.7 1.5 %collective-permute-start.20 = (bf16[32,1536]{1,0:T(8,128)(2,1)S(1)}, bf16[32,1536]{1,0:T(8,128)(2,1)S(1)}, u32[]{:S(2)}, u32[]{:S(2)}) collective-permute-start(bf16[32,1536]{1,0:T(8,128)(2,1)S(1)} %get-tuple-element.101), channel_id=1, source_target_pairs={{0,4},{4,0},{8,12},{12,8},{16,20},{20,16},{24,28},{28,24},{1,5},{5... | collective-permute-start | bytes 294920 | tf_op jit(solution)/shard_map/ppermute | solution.py:271
  90.2 1.2 collective-permute-start.21
  91.4 0.5 collective-permute-start.22
  91.9 2.8 %shard_map.99 = (f32[2,3072,1024]{2,1,0:T(8,128)}, f32[2,3072,1024]{2,1,0:T(8,128)}) custom-call(bf16[2,320,3072]{2,1,0:T(8,128)(2,1)S(1)} %copy-done, bf16[2,320,1024]{2,1,0:T(8,128)(2,1)S(1)} %get-tuple-element.81.gate_grad, bf16[2,320,1024]{2,1,0:T(8,128)(2,1)S(1)} %get-tuple-element.82.up_grad, ...), custom_call_target="tpu_custom_call", output_to_operand_aliasing={{0}: (3, {}), {1}: (4, {})} | custom-call | flops 671088640 | bytes 4194304 | tf_op jit(solution)/shard_map/pallas_call | solution.py:238
  94.7 1.1 collective-permute-done.21
  95.7 0.3 collective-permute-done.22
  96.2 2.6 %collective-permute-start.23 = (bf16[32,3072]{1,0:T(8,128)(2,1)S(1)}, bf16[32,3072]{1,0:T(8,128)(2,1)S(1)}, u32[]{:S(2)}, u32[]{:S(2)}) collective-permute-start(bf16[32,3072]{1,0:T(8,128)(2,1)S(1)} %pad_maximum_fusion.5), channel_id=1, source_target_pairs={{0,16},{4,20},{8,24},{12,28},{16,0},{20,4},{24,8},{28,12},{1,17},{... | collective-permute-start | bytes 589832 | tf_op jit(solution)/shard_map/ppermute | solution.py:271
  98.8 5.5 %shard_map.100 = (f32[2,3072,1024]{2,1,0:T(8,128)}, f32[2,3072,1024]{2,1,0:T(8,128)}) custom-call(bf16[2,320,3072]{2,1,0:T(8,128)(2,1)S(1)} %copy-done, bf16[2,320,1024]{2,1,0:T(8,128)(2,1)S(1)} %get-tuple-element.81.gate_grad, bf16[2,320,1024]{2,1,0:T(8,128)(2,1)S(1)} %get-tuple-element.82.up_grad, ...), custom_call_target="tpu_custom_call", output_to_operand_aliasing={{0}: (3, {}), {1}: (4, {})} | custom-call | flops 2013265920 | bytes 12582912 | tf_op jit(solution)/shard_map/pallas_call | solution.py:238
  104.3 1.8 %collective-permute-done.23 = bf16[32,3072]{1,0:T(8,128)(2,1)S(1)} collective-permute-done((bf16[32,3072]{1,0:T(8,128)(2,1)S(1)}, bf16[32,3072]{1,0:T(8,128)(2,1)S(1)}, u32[]{:S(2)}, u32[]{:S(2)}) %collective-permute-start.23) | collective-permute-done | bytes 196640 | tf_op jit(solution)/shard_map/ppermute | solution.py:271
  106.2 0.5 collective-permute-start.26
  106.7 1.5 %collective-permute-start.25 = (bf16[32,3072]{1,0:T(8,128)(2,1)S(1)}, bf16[32,3072]{1,0:T(8,128)(2,1)S(1)}, u32[]{:S(2)}, u32[]{:S(2)}) collective-permute-start(bf16[32,3072]{1,0:T(8,128)(2,1)S(1)} %add_convert_fusion.2), channel_id=1, source_target_pairs={{0,4},{4,0},{8,12},{12,8},{16,20},{20,16},{24,28},{28,24},{1,5},{5... | collective-permute-start | bytes 589832 | tf_op jit(solution)/shard_map/ppermute | solution.py:271
  108.2 1.5 %collective-permute-start.24 = (bf16[32,3072]{1,0:T(8,128)(2,1)S(1)}, bf16[32,3072]{1,0:T(8,128)(2,1)S(1)}, u32[]{:S(2)}, u32[]{:S(2)}) collective-permute-start(bf16[32,3072]{1,0:T(8,128)(2,1)S(1)} %add_convert_fusion.2), channel_id=1, source_target_pairs={{0,8},{4,12},{8,0},{12,4},{16,24},{20,28},{24,16},{28,20},{1,9},{5... | collective-permute-start | bytes 589832 | tf_op jit(solution)/shard_map/ppermute | solution.py:271
  109.7 5.5 %shard_map.101 = (f32[2,3072,1024]{2,1,0:T(8,128)}, f32[2,3072,1024]{2,1,0:T(8,128)}) custom-call(bf16[2,320,3072]{2,1,0:T(8,128)(2,1)S(1)} %copy-done, bf16[2,320,1024]{2,1,0:T(8,128)(2,1)S(1)} %get-tuple-element.81.gate_grad, bf16[2,320,1024]{2,1,0:T(8,128)(2,1)S(1)} %get-tuple-element.82.up_grad, ...), custom_call_target="tpu_custom_call", output_to_operand_aliasing={{0}: (3, {}), {1}: (4, {})} | custom-call | flops 2013265920 | bytes 12582912 | tf_op jit(solution)/shard_map/pallas_call | solution.py:238
  115.2 1.6 %collective-permute-done.25 = bf16[32,3072]{1,0:T(8,128)(2,1)S(1)} collective-permute-done((bf16[32,3072]{1,0:T(8,128)(2,1)S(1)}, bf16[32,3072]{1,0:T(8,128)(2,1)S(1)}, u32[]{:S(2)}, u32[]{:S(2)}) %collective-permute-start.25) | collective-permute-done | bytes 196640 | tf_op jit(solution)/shard_map/ppermute | solution.py:271
  117.0 1.0 reverse_select_fusion
  (61 shorter events, 2.0 us)
Async XLA Ops:
  1.8 16.2 %collective-permute-start = (bf16[128,3072]{1,0:T(8,128)(2,1)}, bf16[128,3072]{1,0:T(8,128)(2,1)S(1)}, u32[]{:S(2)}, u32[]{:S(2)}) collective-permute-start(bf16[128,3072]{1,0:T(8,128)(2,1)} %refs_0_), channel_id=1, source_target_pairs={{0,1},{1,0},{2,3},{3,2},{4,5},{5,4},{6,7},{7,6},{8,9},{9,8},{10,11... | collective-permute-start | bytes 2359304 | tf_op jit(solution)/shard_map/ppermute | solution.py:271
  2.3 12.3 %collective-permute-start.5 = (bf16[64,3072]{1,0:T(8,128)(2,1)S(1)}, bf16[64,3072]{1,0:T(8,128)(2,1)S(1)}, u32[]{:S(2)}, u32[]{:S(2)}) collective-permute-start(bf16[64,3072]{1,0:T(8,128)(2,1)S(1)} %pad_maximum_fusion.1), channel_id=1, source_target_pairs={{0,2},{1,3},{2,0},{3,1},{4,6},{5,7},{6,4},{7,5},{8,10},{9,11},{10,... | collective-permute-start | bytes 1179656 | tf_op jit(solution)/shard_map/ppermute | solution.py:271
  14.6 6.9 %collective-permute-start.7 = (bf16[32,3072]{1,0:T(8,128)(2,1)S(1)}, bf16[32,3072]{1,0:T(8,128)(2,1)S(1)}, u32[]{:S(2)}, u32[]{:S(2)}) collective-permute-start(bf16[32,3072]{1,0:T(8,128)(2,1)S(1)} %slice.136), channel_id=1, source_target_pairs={{0,8},{4,12},{8,0},{12,4},{16,24},{20,28},{24,16},{28,20},{1,9},{5... | collective-permute-start | bytes 589832 | tf_op jit(solution)/shard_map/ppermute | solution.py:271
  16.5 6.2 %collective-permute-start.6 = (bf16[32,3072]{1,0:T(8,128)(2,1)S(1)}, bf16[32,3072]{1,0:T(8,128)(2,1)S(1)}, u32[]{:S(2)}, u32[]{:S(2)}) collective-permute-start(bf16[32,3072]{1,0:T(8,128)(2,1)S(1)} %slice.136), channel_id=1, source_target_pairs={{0,4},{4,0},{8,12},{12,8},{16,20},{20,16},{24,28},{28,24},{1,5},{5... | collective-permute-start | bytes 589832 | tf_op jit(solution)/shard_map/ppermute | solution.py:271
  18.0 3.5 %copy-start.2 = (bf16[128,3072]{1,0:T(8,128)(2,1)}, bf16[128,3072]{1,0:T(8,128)(2,1)S(1)}, u32[]{:S(2)}) copy-start(bf16[128,3072]{1,0:T(8,128)(2,1)S(1)} %collective-permute-done.refs_1_) | copy-start | bytes 2359300
  19.5 3.1 %collective-permute-start.1 = (f32[2,2,128]{2,0,1:T(2,128)S(1)}, f32[2,2,128]{2,0,1:T(2,128)S(1)}, u32[]{:S(2)}, u32[]{:S(2)}) collective-permute-start(f32[2,2,128]{2,0,1:T(2,128)S(1)} %get-tuple-element.151), channel_id=1, source_target_pairs={{0,1},{1,0},{2,3},{3,2},{4,5},{5,4},{6,7},{7,6},{8,9},{9,8},{10,11... | collective-permute-start | bytes 6152 | tf_op jit(solution)/shard_map/ppermute | solution.py:271
  19.6 4.6 %collective-permute-start.2 = (f32[2,2,128]{2,0,1:T(2,128)S(1)}, f32[2,2,128]{2,0,1:T(2,128)S(1)}, u32[]{:S(2)}, u32[]{:S(2)}) collective-permute-start(f32[2,2,128]{2,0,1:T(2,128)S(1)} %get-tuple-element.152), channel_id=1, source_target_pairs={{0,2},{1,3},{2,0},{3,1},{4,6},{5,7},{6,4},{7,5},{8,10},{9,11},{10,... | collective-permute-start | bytes 6152 | tf_op jit(solution)/shard_map/ppermute | solution.py:271
  21.2 3.2 %collective-permute-start.3 = (f32[2,2,128]{2,0,1:T(2,128)S(1)}, f32[2,2,128]{2,0,1:T(2,128)S(1)}, u32[]{:S(2)}, u32[]{:S(2)}) collective-permute-start(f32[2,2,128]{2,0,1:T(2,128)S(1)} %get-tuple-element.153), channel_id=1, source_target_pairs={{0,3},{1,2},{2,1},{3,0},{4,7},{5,6},{6,5},{7,4},{8,11},{9,10},{10,... | collective-permute-start | bytes 6152 | tf_op jit(solution)/shard_map/ppermute | solution.py:271
  21.5 21.4 %collective-permute-start.4 = (bf16[128,3072]{1,0:T(8,128)(2,1)}, bf16[128,3072]{1,0:T(8,128)(2,1)S(1)}, u32[]{:S(2)}, u32[]{:S(2)}) collective-permute-start(bf16[128,3072]{1,0:T(8,128)(2,1)} %refs_0_.1), channel_id=1, source_target_pairs={{0,1},{1,0},{2,3},{3,2},{4,5},{5,4},{6,7},{7,6},{8,9},{9,8},{10,11... | collective-permute-start | bytes 2359304 | tf_op jit(solution)/shard_map/ppermute | solution.py:271
  22.7 3.3 %collective-permute-start.8 = (bf16[64,3072]{1,0:T(8,128)(2,1)S(1)}, bf16[64,3072]{1,0:T(8,128)(2,1)S(1)}, u32[]{:S(2)}, u32[]{:S(2)}) collective-permute-start(bf16[64,3072]{1,0:T(8,128)(2,1)S(1)} %collective-permute-done.5.refs_2_), channel_id=1, source_target_pairs={{0,1},{1,0},{2,3},{3,2},{4,5},{5,4},{6,7},{7,6},{8,9},{9,8},{10,11... | collective-permute-start | bytes 1179656 | tf_op jit(solution)/shard_map/ppermute | solution.py:271
  22.7 20.2 %collective-permute-start.11 = (bf16[128,3072]{1,0:T(8,128)(2,1)}, bf16[128,3072]{1,0:T(8,128)(2,1)S(1)}, u32[]{:S(2)}, u32[]{:S(2)}) collective-permute-start(bf16[128,3072]{1,0:T(8,128)(2,1)} %refs_0_.1), channel_id=1, source_target_pairs={{0,2},{1,3},{2,0},{3,1},{4,6},{5,7},{6,4},{7,5},{8,10},{9,11},{10,... | collective-permute-start | bytes 2359304 | tf_op jit(solution)/shard_map/ppermute | solution.py:271
  24.2 1.6 %collective-permute-start.10 = (bf16[32,3072]{1,0:T(8,128)(2,1)S(1)}, bf16[32,3072]{1,0:T(8,128)(2,1)S(1)}, u32[]{:S(2)}, u32[]{:S(2)}) collective-permute-start(bf16[32,3072]{1,0:T(8,128)(2,1)S(1)} %collective-permute-done.7.refs_4_), channel_id=1, source_target_pairs={{0,1},{1,0},{2,3},{3,2},{4,5},{5,4},{6,7},{7,6},{8,9},{9,8},{10,11... | collective-permute-start | bytes 589832 | tf_op jit(solution)/shard_map/ppermute | solution.py:271
  24.4 1.5 %collective-permute-start.9 = (bf16[32,3072]{1,0:T(8,128)(2,1)S(1)}, bf16[32,3072]{1,0:T(8,128)(2,1)S(1)}, u32[]{:S(2)}, u32[]{:S(2)}) collective-permute-start(bf16[32,3072]{1,0:T(8,128)(2,1)S(1)} %collective-permute-done.6.refs_3_), channel_id=1, source_target_pairs={{0,1},{1,0},{2,3},{3,2},{4,5},{5,4},{6,7},{7,6},{8,9},{9,8},{10,11... | collective-permute-start | bytes 589832 | tf_op jit(solution)/shard_map/ppermute | solution.py:271
  25.7 19.4 %copy-start.1 = (bf16[128,3072]{1,0:T(8,128)(2,1)S(1)}, bf16[128,3072]{1,0:T(8,128)(2,1)}, u32[]{:S(2)}) copy-start(bf16[128,3072]{1,0:T(8,128)(2,1)} %refs_0_.1) | copy-start | bytes 2359300
  42.8 2.3 %collective-permute-start.12 = (bf16[128,3072]{1,0:T(8,128)(2,1)S(1)}, bf16[128,3072]{1,0:T(8,128)(2,1)S(1)}, u32[]{:S(2)}, u32[]{:S(2)}) collective-permute-start(bf16[128,3072]{1,0:T(8,128)(2,1)S(1)} %collective-permute-done.11.refs_2_), channel_id=1, source_target_pairs={{0,1},{1,0},{2,3},{3,2},{4,5},{5,4},{6,7},{7,6},{8,9},{9,8},{10,11... | collective-permute-start | bytes 2359304 | tf_op jit(solution)/shard_map/ppermute | solution.py:271
  63.1 8.8 %collective-permute-start.14 = (bf16[256,1536]{1,0:T(8,128)(2,1)S(1)}, bf16[256,1536]{1,0:T(8,128)(2,1)S(1)}, u32[]{:S(2)}, u32[]{:S(2)}) collective-permute-start(bf16[256,1536]{1,0:T(8,128)(2,1)S(1)} %get-tuple-element.86), channel_id=1, source_target_pairs={{0,1},{1,0},{2,3},{3,2},{4,5},{5,4},{6,7},{7,6},{8,9},{9,8},{10,11... | collective-permute-start | bytes 2359304 | tf_op jit(solution)/shard_map/ppermute | solution.py:271
  71.5 2.4 %collective-permute-start.13 = (bf16[256,1536]{1,0:T(8,128)(2,1)S(1)}, bf16[256,1536]{1,0:T(8,128)(2,1)S(1)}, u32[]{:S(2)}, u32[]{:S(2)}) collective-permute-start(bf16[256,1536]{1,0:T(8,128)(2,1)S(1)} %get-tuple-element.84), channel_id=1, source_target_pairs={{0,1},{1,0},{2,3},{3,2},{4,5},{5,4},{6,7},{7,6},{8,9},{9,8},{10,11... | collective-permute-start | bytes 2359304 | tf_op jit(solution)/shard_map/ppermute | solution.py:271
  71.9 7.2 %copy-start = (bf16[2,320,3072]{2,1,0:T(8,128)(2,1)S(1)}, bf16[2,320,3072]{2,1,0:T(8,128)(2,1)}, u32[]{:S(2)}) copy-start(bf16[2,320,3072]{2,1,0:T(8,128)(2,1)} %get-tuple-element.121.rows) | copy-start | bytes 11796484
  74.0 13.6 %collective-permute-start.15 = (bf16[128,1536]{1,0:T(8,128)(2,1)S(1)}, bf16[128,1536]{1,0:T(8,128)(2,1)S(1)}, u32[]{:S(2)}, u32[]{:S(2)}) collective-permute-start(bf16[128,1536]{1,0:T(8,128)(2,1)S(1)} %slice.180), channel_id=1, source_target_pairs={{0,2},{1,3},{2,0},{3,1},{4,6},{5,7},{6,4},{7,5},{8,10},{9,11},{10,... | collective-permute-start | bytes 1179656 | tf_op jit(solution)/shard_map/ppermute | solution.py:271
  75.6 11.7 %collective-permute-start.16 = (bf16[64,1536]{1,0:T(8,128)(2,1)S(1)}, bf16[64,1536]{1,0:T(8,128)(2,1)S(1)}, u32[]{:S(2)}, u32[]{:S(2)}) collective-permute-start(bf16[64,1536]{1,0:T(8,128)(2,1)S(1)} %pad_maximum_fusion.2), channel_id=1, source_target_pairs={{0,8},{4,12},{8,0},{12,4},{16,24},{20,28},{24,16},{28,20},{1,9},{5... | collective-permute-start | bytes 589832 | tf_op jit(solution)/shard_map/ppermute | solution.py:271
  76.1 11.3 %collective-permute-start.17 = (bf16[64,1536]{1,0:T(8,128)(2,1)S(1)}, bf16[64,1536]{1,0:T(8,128)(2,1)S(1)}, u32[]{:S(2)}, u32[]{:S(2)}) collective-permute-start(bf16[64,1536]{1,0:T(8,128)(2,1)S(1)} %pad_maximum_fusion.3), channel_id=1, source_target_pairs={{0,4},{4,0},{8,12},{12,8},{16,20},{20,16},{24,28},{28,24},{1,5},{5... | collective-permute-start | bytes 589832 | tf_op jit(solution)/shard_map/ppermute | solution.py:271
  77.6 10.1 %collective-permute-start.18 = (bf16[64,1536]{1,0:T(8,128)(2,1)S(1)}, bf16[64,1536]{1,0:T(8,128)(2,1)S(1)}, u32[]{:S(2)}, u32[]{:S(2)}) collective-permute-start(bf16[64,1536]{1,0:T(8,128)(2,1)S(1)} %pad_maximum_fusion.4), channel_id=1, source_target_pairs={{0,12},{4,8},{8,4},{12,0},{16,28},{20,24},{24,20},{28,16},{1,13},{... | collective-permute-start | bytes 589832 | tf_op jit(solution)/shard_map/ppermute | solution.py:271
  87.8 6.8 %collective-permute-start.19 = (bf16[32,1536]{1,0:T(8,128)(2,1)S(1)}, bf16[32,1536]{1,0:T(8,128)(2,1)S(1)}, u32[]{:S(2)}, u32[]{:S(2)}) collective-permute-start(bf16[32,1536]{1,0:T(8,128)(2,1)S(1)} %get-tuple-element.100), channel_id=1, source_target_pairs={{0,8},{4,12},{8,0},{12,4},{16,24},{20,28},{24,16},{28,20},{1,9},{5... | collective-permute-start | bytes 294920 | tf_op jit(solution)/shard_map/ppermute | solution.py:271
  88.7 6.0 %collective-permute-start.20 = (bf16[32,1536]{1,0:T(8,128)(2,1)S(1)}, bf16[32,1536]{1,0:T(8,128)(2,1)S(1)}, u32[]{:S(2)}, u32[]{:S(2)}) collective-permute-start(bf16[32,1536]{1,0:T(8,128)(2,1)S(1)} %get-tuple-element.101), channel_id=1, source_target_pairs={{0,4},{4,0},{8,12},{12,8},{16,20},{20,16},{24,28},{28,24},{1,5},{5... | collective-permute-start | bytes 294920 | tf_op jit(solution)/shard_map/ppermute | solution.py:271
  90.2 5.5 %collective-permute-start.21 = (bf16[32,1536]{1,0:T(8,128)(2,1)S(1)}, bf16[32,1536]{1,0:T(8,128)(2,1)S(1)}, u32[]{:S(2)}, u32[]{:S(2)}) collective-permute-start(bf16[32,1536]{1,0:T(8,128)(2,1)S(1)} %get-tuple-element.102), channel_id=1, source_target_pairs={{0,12},{4,8},{8,4},{12,0},{16,28},{20,24},{24,20},{28,16},{1,13},{... | collective-permute-start | bytes 294920 | tf_op jit(solution)/shard_map/ppermute | solution.py:271
  91.4 4.6 %collective-permute-start.22 = (bf16[32,1536]{1,0:T(8,128)(2,1)S(1)}, bf16[32,1536]{1,0:T(8,128)(2,1)S(1)}, u32[]{:S(2)}, u32[]{:S(2)}) collective-permute-start(bf16[32,1536]{1,0:T(8,128)(2,1)S(1)} %add_convert_fusion.11), channel_id=1, source_target_pairs={{0,2},{1,3},{2,0},{3,1},{4,6},{5,7},{6,4},{7,5},{8,10},{9,11},{10,... | collective-permute-start | bytes 294920 | tf_op jit(solution)/shard_map/ppermute | solution.py:271
  96.2 9.9 %collective-permute-start.23 = (bf16[32,3072]{1,0:T(8,128)(2,1)S(1)}, bf16[32,3072]{1,0:T(8,128)(2,1)S(1)}, u32[]{:S(2)}, u32[]{:S(2)}) collective-permute-start(bf16[32,3072]{1,0:T(8,128)(2,1)S(1)} %pad_maximum_fusion.5), channel_id=1, source_target_pairs={{0,16},{4,20},{8,24},{12,28},{16,0},{20,4},{24,8},{28,12},{1,17},{... | collective-permute-start | bytes 589832 | tf_op jit(solution)/shard_map/ppermute | solution.py:271
  106.2 9.1 %collective-permute-start.26 = (bf16[32,3072]{1,0:T(8,128)(2,1)S(1)}, bf16[32,3072]{1,0:T(8,128)(2,1)S(1)}, u32[]{:S(2)}, u32[]{:S(2)}) collective-permute-start(bf16[32,3072]{1,0:T(8,128)(2,1)S(1)} %add_convert_fusion.2), channel_id=1, source_target_pairs={{0,12},{4,8},{8,4},{12,0},{16,28},{20,24},{24,20},{28,16},{1,13},{... | collective-permute-start | bytes 589832 | tf_op jit(solution)/shard_map/ppermute | solution.py:271
  106.7 10.1 %collective-permute-start.25 = (bf16[32,3072]{1,0:T(8,128)(2,1)S(1)}, bf16[32,3072]{1,0:T(8,128)(2,1)S(1)}, u32[]{:S(2)}, u32[]{:S(2)}) collective-permute-start(bf16[32,3072]{1,0:T(8,128)(2,1)S(1)} %add_convert_fusion.2), channel_id=1, source_target_pairs={{0,4},{4,0},{8,12},{12,8},{16,20},{20,16},{24,28},{28,24},{1,5},{5... | collective-permute-start | bytes 589832 | tf_op jit(solution)/shard_map/ppermute | solution.py:271
  108.2 8.6 %collective-permute-start.24 = (bf16[32,3072]{1,0:T(8,128)(2,1)S(1)}, bf16[32,3072]{1,0:T(8,128)(2,1)S(1)}, u32[]{:S(2)}, u32[]{:S(2)}) collective-permute-start(bf16[32,3072]{1,0:T(8,128)(2,1)S(1)} %add_convert_fusion.2), channel_id=1, source_target_pairs={{0,8},{4,12},{8,0},{12,4},{16,24},{20,28},{24,16},{28,20},{1,9},{5... | collective-permute-start | bytes 589832 | tf_op jit(solution)/shard_map/ppermute | solution.py:271
where the time goes:
time: 118 us
  Pallas kernels  64 us (54%)
  starting transfers between devices  26.8 us (23%)
  waiting for transfers between devices  20.7 us (18%)
  other arithmetic  3.88 us (3%)
  local copies, waits for them, and re-layouts  1.55 us (1%)
    ppermute x27, starting transfers between devices, flip(): return lax.ppermute(value, axis, [(i, i ^ bit) for i in range(count)])  26.8 us
    pallas_call x4, Pallas kernels, weight_grads(): pl.pallas_call(weights_kernel, grid=(steps,), in_specs=[pl.BlockSpec((1,...  22 us
    ppermute x27, waiting for transfers between devices, flip(): return lax.ppermute(value, axis, [(i, i ^ bit) for i in range(count)])  20.7 us
    pallas_call x2, Pallas kernels, input_sums(): pl.pallas_call(functools.partial(inputs_kernel, groups), grid=(steps,), i...  16.2 us
    pallas_call x1, Pallas kernels, forward(): pl.pallas_call(functools.partial(forward_kernel, len(pieces)), grid=(expe...  15.9 us
    pallas_call x1, Pallas kernels, hidden_grads(): pl.pallas_call(functools.partial(hidden_kernel, len(pieces)), grid=(exper...  9.87 us
  transfers between devices with their start and end apart: 27, of which 11 were waited for; matrix products, arithmetic and copies ran while one was open for 2% of the time, Pallas kernels for 39%

commit v1 on v0

--- a/solution.py
+++ b/solution.py
@@ -227,19 +227,21 @@
     grad_up[0] = dot(rows[0], up_grad[0], TN)
 
 
-def weight_grads(rows, gate_grad, up_grad, before, expert, first=0, steps=None):
+def weight_grads(rows, gate_grad, up_grad, before, first, steps):
     experts, slots, features = rows.shape
     units = gate_grad.shape[2]
     wide = FEATURE_TILE
-    steps = features // wide if steps is None else steps
-    unit = pl.BlockSpec((1, slots, units), lambda d: (expert, 0, 0))
-    out = pl.BlockSpec((1, wide, units), lambda d: (expert, first + d, 0))
+    each = features // wide
+    unit = pl.BlockSpec((1, slots, units), lambda i: ((first + i) // each, 0, 0))
+    out = pl.BlockSpec((1, wide, units), lambda i: ((first + i) // each, (first + i) % each, 0))
     kept = [] if before is None else list(before)
     return pl.pallas_call(
         weights_kernel,
         grid=(steps,),
         in_specs=[
-            pl.BlockSpec((1, slots, wide), lambda d: (expert, 0, first + d)), unit, unit
+            pl.BlockSpec((1, slots, wide), lambda i: ((first + i) // each, 0, (first + i) % each)),
+            unit,
+            unit,
         ]
         + [pl.BlockSpec(memory_space=pl.ANY)] * len(kept),
         out_specs=[out, out],
@@ -301,13 +303,11 @@
     def to_core(values):
         return tuple(flip(v, "expert", 1) for v in values)
 
-    x_mine = jnp.concatenate(
-        [quarters(layer_input, tokens, q) for q in (corner, 3 - corner)], axis=0
-    )
-    x_mine, layer_input, out_grad, routes = lax.optimization_barrier(
-        (x_mine, layer_input, out_grad, routes)
-    )
-    x_across = flip(x_mine, "expert", 2)
+    x_mine = [quarters(layer_input, tokens, q) for q in (corner, 3 - corner)]
+    *x_mine, layer_input, out_grad, routes = lax.optimization_barrier(
+        (*x_mine, layer_input, out_grad, routes)
+    )
+    x_across, x_corner = [flip(v, "expert", 2) for v in x_mine]
     x_sibling, g_sibling = to_core((layer_input, out_grad))
     x_sibling, routes = lax.optimization_barrier((x_sibling, routes))
     table = route_table(routes, gate_values)
@@ -315,8 +315,8 @@
     for r in range(4):
         part = lax.dynamic_slice_in_dim(table, (me ^ r) * experts, experts, 0)
         tables.append(flip(part, "expert", r) if r > 0 else part)
-    x_across, g_own = lax.optimization_barrier((x_across, out_grad))
-    x_far = (x_across, flip(x_across[:quarter], "dp", 1), flip(x_across[:quarter], "dp", 2))
+    x_corner, g_own = lax.optimization_barrier((x_corner, out_grad))
+    x_far = (x_across, x_corner, flip(x_across, "dp", 1), flip(x_across, "dp", 2))
     g_across = flip(g_own, "expert", 2)
     x_far = (*x_far, *to_core(x_far))
     table = jnp.stack(tables, axis=2)
@@ -351,21 +351,21 @@
     chip_b = [add(a, b) for a, b in zip(cut(kept_b, 8), cut(got, 8))]
     far_a = chip_a[tokens:]
     away = [jnp.concatenate([chip_b[q], chip_b[4 + q]], axis=0) for q in (1, 2, 3)]
-    (far_a, *away), grads = piece((far_a, *away), None, 0, 0, 5)
+    (far_a, *away), grads = piece((far_a, *away), None, 0, 3)
     got_a, got_b = flip(far_a, "expert", 2), corners(away)
     got_a, got_b, *grads = lax.optimization_barrier((got_a, got_b, *grads))
     own_a = [add(a, b) for a, b in zip(cut(chip_a, 4), cut(got_a, 4))]
     mine_b = add(chip_b[0], *(v[:quarter] for v in got_b))
     far_b = add(chip_b[4], *(v[quarter:] for v in got_b))
-    (far_b, *own_a), grads = piece((far_b, *own_a), grads, 0, 5, 1)
+    (far_b, *own_a), grads = piece((far_b, *own_a), grads, 3, 2)
     got_a, got_b = corners(own_a[1:]), flip(far_b, "expert", 2)
     got_a, got_b, *grads = lax.optimization_barrier((got_a, got_b, *grads))
     mine = jnp.concatenate([add(own_a[0], *got_a), add(mine_b, got_b)], axis=1)
-    mine, grads = piece(mine, grads, 1, 0, 3)
+    mine, grads = piece(mine, grads, 5, 4)
     got = flip(mine, "dp", 4)
     got, *grads = lax.optimization_barrier((got, *grads))
     mine = add(mine, got)
-    mine, grads = piece(mine, grads, 1, 3, 3)
+    mine, grads = piece(mine, grads, 9, 3)
     got = corners([mine] * 3)
     got, *grads = lax.optimization_barrier((got, *grads))
     total = swap_order(jnp.concatenate([mine, *got], axis=0), side, pair, 0)
@@ -384,9 +384,8 @@
     gate_grad, up_grad = hidden_grads([grads_in], slot, weight, act, slope, w_down)
     groups = (tuple(range(slot.shape[1])),)
     (sums,) = input_sums(back_matrix(slot), gate_grad, up_grad, w_gate, w_up, groups, 0, 1)
-    grads = None
-    for l in range(experts):
-        grads = weight_grads(rows, gate_grad, up_grad, grads, l)
+    blocks = experts * layer_input.shape[1] // FEATURE_TILE
+    grads = weight_grads(rows, gate_grad, up_grad, None, 0, blocks)
     own = lax.psum_scatter(sums, "expert", scatter_dimension=0, tiled=True)
     return (lax.psum(own, "dp"), *grads)
 

time: 118 us -> 113 us (0.958)
  waiting for transfers between devices: 20.7 us -> 14.8 us
    ppermute x27 -> x29, waiting for transfers between devices: 20.7 us -> 14.8 us  [flip(): return lax.ppermute(value, axis, [(i, i ^ bit) for i in range(count)])]
    ppermute x27 -> x29, starting transfers between devices: 26.8 us -> 27.9 us  [flip(): return lax.ppermute(value, axis, [(i, i ^ bit) for i in range(count)])]
  transfers between devices with their start and end apart: 27 -> 29, of which waited for: 11 -> 7; matrix products, arithmetic and copies ran while one was open for 2% -> 2% of each run, Pallas kernels for 39% -> 41%
where the time goes in v1:
time: 113 us
  Pallas kernels  64 us (57%)
  starting transfers between devices  27.9 us (25%)
  waiting for transfers between devices  14.8 us (13%)
  other arithmetic  3.85 us (3%)
  local copies, waits for them, and re-layouts  1.54 us (1%)
    ppermute x29, starting transfers between devices, flip(): return lax.ppermute(value, axis, [(i, i ^ bit) for i in range(count)])  27.9 us
    pallas_call x4, Pallas kernels, weight_grads(): pl.pallas_call(weights_kernel, grid=(steps,), in_specs=[pl.BlockSpec((1,...  22 us
    pallas_call x2, Pallas kernels, input_sums(): pl.pallas_call(functools.partial(inputs_kernel, groups), grid=(steps,), i...  16.2 us
    pallas_call x1, Pallas kernels, forward(): pl.pallas_call(functools.partial(forward_kernel, len(pieces)), grid=(expe...  15.9 us
    ppermute x29, waiting for transfers between devices, flip(): return lax.ppermute(value, axis, [(i, i ^ bit) for i in range(count)])  14.8 us
    pallas_call x1, Pallas kernels, hidden_grads(): pl.pallas_call(functools.partial(hidden_kernel, len(pieces)), grid=(exper...  9.88 us
  transfers between devices with their start and end apart: 29, of which 7 were waited for; matrix products, arithmetic and copies ran while one was open for 2% of the time, Pallas kernels for 41%

profile of v1, /device:TPU:0, one launch (start us, length us, event | category | flops | bytes accessed | tf_op | source)
XLA Modules:
  0.0 113.2 jit_solution(1588326506276454629)
XLA Ops:
  0.7 1.1 constant_dynamic-slice_fusion
  1.7 0.5 collective-permute-start
  2.3 2.6 %collective-permute-start.5 = (bf16[32,3072]{1,0:T(8,128)(2,1)S(1)}, bf16[32,3072]{1,0:T(8,128)(2,1)S(1)}, u32[]{:S(2)}, u32[]{:S(2)}) collective-permute-start(bf16[32,3072]{1,0:T(8,128)(2,1)S(1)} %get-tuple-element.74), channel_id=1, source_target_pairs={{0,2},{1,3},{2,0},{3,1},{4,6},{5,7},{6,4},{7,5},{8,10},{9,11},{10,... | collective-permute-start | bytes 589832 | tf_op jit(solution)/shard_map/ppermute | solution.py:273
  4.9 5.7 %collective-permute-done.5.refs_2_ = bf16[32,3072]{1,0:T(8,128)(2,1)S(1)} collective-permute-done((bf16[32,3072]{1,0:T(8,128)(2,1)S(1)}, bf16[32,3072]{1,0:T(8,128)(2,1)S(1)}, u32[]{:S(2)}, u32[]{:S(2)}) %collective-permute-start.5) | collective-permute-done | bytes 196640 | tf_op jit(solution)/shard_map/ppermute | solution.py:273
  10.6 2.0 %collective-permute-start.8 = (bf16[32,3072]{1,0:T(8,128)(2,1)S(1)}, bf16[32,3072]{1,0:T(8,128)(2,1)S(1)}, u32[]{:S(2)}, u32[]{:S(2)}) collective-permute-start(bf16[32,3072]{1,0:T(8,128)(2,1)S(1)} %collective-permute-done.5.refs_2_), channel_id=1, source_target_pairs={{0,8},{4,12},{8,0},{12,4},{16,24},{20,28},{24,16},{28,20},{1,9},{5... | collective-permute-start | bytes 589832 | tf_op jit(solution)/shard_map/ppermute | solution.py:273
  12.6 1.5 %collective-permute-start.7 = (bf16[32,3072]{1,0:T(8,128)(2,1)S(1)}, bf16[32,3072]{1,0:T(8,128)(2,1)S(1)}, u32[]{:S(2)}, u32[]{:S(2)}) collective-permute-start(bf16[32,3072]{1,0:T(8,128)(2,1)S(1)} %collective-permute-done.5.refs_2_), channel_id=1, source_target_pairs={{0,4},{4,0},{8,12},{12,8},{16,20},{20,16},{24,28},{28,24},{1,5},{5... | collective-permute-start | bytes 589832 | tf_op jit(solution)/shard_map/ppermute | solution.py:273
  14.1 0.7 fusion.1
  14.9 0.7 select_reduce_fusion
  15.7 1.6 %collective-permute-start.2 = (f32[2,2,128]{2,0,1:T(2,128)S(1)}, f32[2,2,128]{2,0,1:T(2,128)S(1)}, u32[]{:S(2)}, u32[]{:S(2)}) collective-permute-start(f32[2,2,128]{2,0,1:T(2,128)S(1)} %get-tuple-element.154), channel_id=1, source_target_pairs={{0,2},{1,3},{2,0},{3,1},{4,6},{5,7},{6,4},{7,5},{8,10},{9,11},{10,... | collective-permute-start | bytes 6152 | tf_op jit(solution)/shard_map/ppermute | solution.py:273
  17.3 0.3 collective-permute-start.3
  17.6 0.3 collective-permute-start.10
  17.9 0.4 collective-permute-done.7.refs_4_
  18.3 1.5 %collective-permute-start.13 = (bf16[128,3072]{1,0:T(8,128)(2,1)}, bf16[128,3072]{1,0:T(8,128)(2,1)S(1)}, u32[]{:S(2)}, u32[]{:S(2)}) collective-permute-start(bf16[128,3072]{1,0:T(8,128)(2,1)} %refs_0_.1), channel_id=1, source_target_pairs={{0,2},{1,3},{2,0},{3,1},{4,6},{5,7},{6,4},{7,5},{8,10},{9,11},{10,... | collective-permute-start | bytes 2359304 | tf_op jit(solution)/shard_map/ppermute | solution.py:273
  19.9 0.5 collective-permute-start.12
  21.1 0.2 iota_compare_fusion
  21.3 0.2 add_convert_fusion.1.back
  21.5 0.5 collective-permute-start.4
  22.0 15.9 %shard_map.94 = (bf16[2,320,3072]{2,1,0:T(8,128)(2,1)}, f32[2,320,1024]{2,1,0:T(8,128)}, f32[2,320,1024]{2,1,0:T(8,128)}) custom-call(bf16[128,3072]{1,0:T(8,128)(2,1)} %refs_0_, bf16[128,3072]{1,0:T(8,128)(2,1)} %copy-done.2, bf16[32,3072]{1,0:T(8,128)(2,1)S(1)} %collective-permute-done.5.refs_2_, bf16[32,3072]{1,0:T(8,128)(2,1)S(1)} %collective-permute-done.6.refs_3_, ...), custom_call_target="tpu_custom_call" | custom-call | flops 8053063680 | bytes 25165824 | tf_op jit(solution)/shard_map/pallas_call | solution.py:121
  38.0 0.2 collective-permute-start.14
  38.1 2.2 %collective-permute-done.14.refs_3_ = bf16[128,3072]{1,0:T(8,128)(2,1)S(1)} collective-permute-done((bf16[128,3072]{1,0:T(8,128)(2,1)S(1)}, bf16[128,3072]{1,0:T(8,128)(2,1)S(1)}, u32[]{:S(2)}, u32[]{:S(2)}) %collective-permute-start.14) | collective-permute-done | bytes 786464 | tf_op jit(solution)/shard_map/ppermute | solution.py:273
  40.3 9.9 %shard_map.95 = (bf16[2,320,1024]{2,1,0:T(8,128)(2,1)S(1)}, bf16[2,320,1024]{2,1,0:T(8,128)(2,1)S(1)}) custom-call(bf16[128,3072]{1,0:T(8,128)(2,1)S(1)} %copy-done.1, bf16[128,3072]{1,0:T(8,128)(2,1)S(1)} %collective-permute-done.4.refs_1_, bf16[128,3072]{1,0:T(8,128)(2,1)S(1)} %collective-permute-done.13.refs_2_, ...), custom_call_target="tpu_custom_call" | custom-call | flops 4026531840 | bytes 12582912 | tf_op jit(solution)/shard_map/pallas_call | solution.py:162
  50.2 8.1 %shard_map.97 = (bf16[256,1536]{1,0:T(8,128)(2,1)S(1)}, bf16[256,1536]{1,0:T(8,128)(2,1)S(1)}) custom-call(bf16[4,128,160]{2,1,0:T(8,128)(2,1)S(1)} %add_convert_fusion.1.back, bf16[2,320,1024]{2,1,0:T(8,128)(2,1)S(1)} %get-tuple-element.83.gate_grad, bf16[2,320,1024]{2,1,0:T(8,128)(2,1)S(1)} %get-tuple-element.84.up_grad, bf16[2,3072,1024]{2,1,0:T(8,128)(2,1)} %w_gate.3, ...), custom_call_target="tpu_custom_call" | custom-call | flops 4026531840 | bytes 12582912 | tf_op jit(solution)/shard_map/pallas_call | solution.py:199
  58.3 0.2 collective-permute-start.16
  58.5 8.1 %shard_map.96 = (bf16[256,1536]{1,0:T(8,128)(2,1)S(1)}, bf16[256,1536]{1,0:T(8,128)(2,1)S(1)}) custom-call(bf16[4,128,160]{2,1,0:T(8,128)(2,1)S(1)} %add_convert_fusion.1.back, bf16[2,320,1024]{2,1,0:T(8,128)(2,1)S(1)} %get-tuple-element.83.gate_grad, bf16[2,320,1024]{2,1,0:T(8,128)(2,1)S(1)} %get-tuple-element.84.up_grad, bf16[2,3072,1024]{2,1,0:T(8,128)(2,1)} %w_gate.3, ...), custom_call_target="tpu_custom_call" | custom-call | flops 4026531840 | bytes 12582912 | tf_op jit(solution)/shard_map/pallas_call | solution.py:199
  66.6 0.4 collective-permute-start.15
  67.1 0.2 add_convert_fusion
  67.3 1.7 %collective-permute-done.15 = bf16[256,1536]{1,0:T(8,128)(2,1)S(1)} collective-permute-done((bf16[256,1536]{1,0:T(8,128)(2,1)S(1)}, bf16[256,1536]{1,0:T(8,128)(2,1)S(1)}, u32[]{:S(2)}, u32[]{:S(2)}) %collective-permute-start.15) | collective-permute-done | bytes 786464 | tf_op jit(solution)/shard_map/ppermute | solution.py:273
  69.2 1.4 %collective-permute-start.17 = (bf16[128,1536]{1,0:T(8,128)(2,1)S(1)}, bf16[128,1536]{1,0:T(8,128)(2,1)S(1)}, u32[]{:S(2)}, u32[]{:S(2)}) collective-permute-start(bf16[128,1536]{1,0:T(8,128)(2,1)S(1)} %slice.175), channel_id=1, source_target_pairs={{0,2},{1,3},{2,0},{3,1},{4,6},{5,7},{6,4},{7,5},{8,10},{9,11},{10,... | collective-permute-start | bytes 1179656 | tf_op jit(solution)/shard_map/ppermute | solution.py:273
  70.6 1.0 collective-permute-start.18
  71.6 1.5 %collective-permute-start.19 = (bf16[64,1536]{1,0:T(8,128)(2,1)S(1)}, bf16[64,1536]{1,0:T(8,128)(2,1)S(1)}, u32[]{:S(2)}, u32[]{:S(2)}) collective-permute-start(bf16[64,1536]{1,0:T(8,128)(2,1)S(1)} %pad_maximum_fusion.2), channel_id=1, source_target_pairs={{0,4},{4,0},{8,12},{12,8},{16,20},{20,16},{24,28},{28,24},{1,5},{5... | collective-permute-start | bytes 589832 | tf_op jit(solution)/shard_map/ppermute | solution.py:273
  73.1 1.0 collective-permute-start.20
  74.0 5.5 %shard_map.98 = (f32[2,3072,1024]{2,1,0:T(8,128)}, f32[2,3072,1024]{2,1,0:T(8,128)}) custom-call(bf16[2,320,3072]{2,1,0:T(8,128)(2,1)S(1)} %copy-done, bf16[2,320,1024]{2,1,0:T(8,128)(2,1)S(1)} %get-tuple-element.83.gate_grad, bf16[2,320,1024]{2,1,0:T(8,128)(2,1)S(1)} %get-tuple-element.84.up_grad), custom_call_target="tpu_custom_call" | custom-call | flops 2013265920 | bytes 12582912 | tf_op jit(solution)/shard_map/pallas_call | solution.py:238
  79.6 2.8 %collective-permute-done.19 = bf16[64,1536]{1,0:T(8,128)(2,1)S(1)} collective-permute-done((bf16[64,1536]{1,0:T(8,128)(2,1)S(1)}, bf16[64,1536]{1,0:T(8,128)(2,1)S(1)}, u32[]{:S(2)}, u32[]{:S(2)}) %collective-permute-start.19) | collective-permute-done | bytes 196640 | tf_op jit(solution)/shard_map/ppermute | solution.py:273
  82.6 1.3 %collective-permute-start.21 = (bf16[32,1536]{1,0:T(8,128)(2,1)S(1)}, bf16[32,1536]{1,0:T(8,128)(2,1)S(1)}, u32[]{:S(2)}, u32[]{:S(2)}) collective-permute-start(bf16[32,1536]{1,0:T(8,128)(2,1)S(1)} %get-tuple-element.102), channel_id=1, source_target_pairs={{0,8},{4,12},{8,0},{12,4},{16,24},{20,28},{24,16},{28,20},{1,9},{5... | collective-permute-start | bytes 294920 | tf_op jit(solution)/shard_map/ppermute | solution.py:273
  83.8 0.7 collective-permute-start.22
  84.6 1.5 %collective-permute-start.23 = (bf16[32,1536]{1,0:T(8,128)(2,1)S(1)}, bf16[32,1536]{1,0:T(8,128)(2,1)S(1)}, u32[]{:S(2)}, u32[]{:S(2)}) collective-permute-start(bf16[32,1536]{1,0:T(8,128)(2,1)S(1)} %get-tuple-element.104), channel_id=1, source_target_pairs={{0,12},{4,8},{8,4},{12,0},{16,28},{20,24},{24,20},{28,16},{1,13},{... | collective-permute-start | bytes 294920 | tf_op jit(solution)/shard_map/ppermute | solution.py:273
  86.1 0.9 collective-permute-start.24
  87.1 4.1 %shard_map.99 = (f32[2,3072,1024]{2,1,0:T(8,128)}, f32[2,3072,1024]{2,1,0:T(8,128)}) custom-call(bf16[2,320,3072]{2,1,0:T(8,128)(2,1)S(1)} %copy-done, bf16[2,320,1024]{2,1,0:T(8,128)(2,1)S(1)} %get-tuple-element.83.gate_grad, bf16[2,320,1024]{2,1,0:T(8,128)(2,1)S(1)} %get-tuple-element.84.up_grad, ...), custom_call_target="tpu_custom_call", output_to_operand_aliasing={{0}: (3, {}), {1}: (4, {})} | custom-call | flops 1342177280 | bytes 8388608 | tf_op jit(solution)/shard_map/pallas_call | solution.py:238
  91.4 2.7 %collective-permute-start.25 = (bf16[32,3072]{1,0:T(8,128)(2,1)S(1)}, bf16[32,3072]{1,0:T(8,128)(2,1)S(1)}, u32[]{:S(2)}, u32[]{:S(2)}) collective-permute-start(bf16[32,3072]{1,0:T(8,128)(2,1)S(1)} %pad_maximum_fusion.4), channel_id=1, source_target_pairs={{0,16},{4,20},{8,24},{12,28},{16,0},{20,4},{24,8},{28,12},{1,17},{... | collective-permute-start | bytes 589832 | tf_op jit(solution)/shard_map/ppermute | solution.py:273
  94.1 6.8 %shard_map.100 = (f32[2,3072,1024]{2,1,0:T(8,128)}, f32[2,3072,1024]{2,1,0:T(8,128)}) custom-call(bf16[2,320,3072]{2,1,0:T(8,128)(2,1)S(1)} %copy-done, bf16[2,320,1024]{2,1,0:T(8,128)(2,1)S(1)} %get-tuple-element.83.gate_grad, bf16[2,320,1024]{2,1,0:T(8,128)(2,1)S(1)} %get-tuple-element.84.up_grad, ...), custom_call_target="tpu_custom_call", output_to_operand_aliasing={{0}: (3, {}), {1}: (4, {})} | custom-call | flops 2684354560 | bytes 16777216 | tf_op jit(solution)/shard_map/pallas_call | solution.py:238
  100.9 0.6 collective-permute-done.25
  101.5 1.2 %collective-permute-start.28 = (bf16[32,3072]{1,0:T(8,128)(2,1)S(1)}, bf16[32,3072]{1,0:T(8,128)(2,1)S(1)}, u32[]{:S(2)}, u32[]{:S(2)}) collective-permute-start(bf16[32,3072]{1,0:T(8,128)(2,1)S(1)} %add_convert_fusion.2), channel_id=1, source_target_pairs={{0,12},{4,8},{8,4},{12,0},{16,28},{20,24},{24,20},{28,16},{1,13},{... | collective-permute-start | bytes 589832 | tf_op jit(solution)/shard_map/ppermute | solution.py:273
  102.8 0.5 collective-permute-start.27
  103.3 1.8 %collective-permute-start.26 = (bf16[32,3072]{1,0:T(8,128)(2,1)S(1)}, bf16[32,3072]{1,0:T(8,128)(2,1)S(1)}, u32[]{:S(2)}, u32[]{:S(2)}) collective-permute-start(bf16[32,3072]{1,0:T(8,128)(2,1)S(1)} %add_convert_fusion.2), channel_id=1, source_target_pairs={{0,8},{4,12},{8,0},{12,4},{16,24},{20,28},{24,16},{28,20},{1,9},{5... | collective-permute-start | bytes 589832 | tf_op jit(solution)/shard_map/ppermute | solution.py:273
  105.1 5.5 %shard_map.101 = (f32[2,3072,1024]{2,1,0:T(8,128)}, f32[2,3072,1024]{2,1,0:T(8,128)}) custom-call(bf16[2,320,3072]{2,1,0:T(8,128)(2,1)S(1)} %copy-done, bf16[2,320,1024]{2,1,0:T(8,128)(2,1)S(1)} %get-tuple-element.83.gate_grad, bf16[2,320,1024]{2,1,0:T(8,128)(2,1)S(1)} %get-tuple-element.84.up_grad, ...), custom_call_target="tpu_custom_call", output_to_operand_aliasing={{0}: (3, {}), {1}: (4, {})} | custom-call | flops 2013265920 | bytes 12582912 | tf_op jit(solution)/shard_map/pallas_call | solution.py:238
  110.6 1.4 %collective-permute-done.27 = bf16[32,3072]{1,0:T(8,128)(2,1)S(1)} collective-permute-done((bf16[32,3072]{1,0:T(8,128)(2,1)S(1)}, bf16[32,3072]{1,0:T(8,128)(2,1)S(1)}, u32[]{:S(2)}, u32[]{:S(2)}) %collective-permute-start.27) | collective-permute-done | bytes 196640 | tf_op jit(solution)/shard_map/ppermute | solution.py:273
  112.1 0.1 reverse_select_fusion.1
  112.2 1.0 reverse_select_fusion
  (63 shorter events, 1.6 us)
Async XLA Ops:
  1.7 12.4 %collective-permute-start = (bf16[128,3072]{1,0:T(8,128)(2,1)}, bf16[128,3072]{1,0:T(8,128)(2,1)S(1)}, u32[]{:S(2)}, u32[]{:S(2)}) collective-permute-start(bf16[128,3072]{1,0:T(8,128)(2,1)} %refs_0_), channel_id=1, source_target_pairs={{0,1},{1,0},{2,3},{3,2},{4,5},{5,4},{6,7},{7,6},{8,9},{9,8},{10,11... | collective-permute-start | bytes 2359304 | tf_op jit(solution)/shard_map/ppermute | solution.py:273
  2.3 8.4 %collective-permute-start.5 = (bf16[32,3072]{1,0:T(8,128)(2,1)S(1)}, bf16[32,3072]{1,0:T(8,128)(2,1)S(1)}, u32[]{:S(2)}, u32[]{:S(2)}) collective-permute-start(bf16[32,3072]{1,0:T(8,128)(2,1)S(1)} %get-tuple-element.74), channel_id=1, source_target_pairs={{0,2},{1,3},{2,0},{3,1},{4,6},{5,7},{6,4},{7,5},{8,10},{9,11},{10,... | collective-permute-start | bytes 589832 | tf_op jit(solution)/shard_map/ppermute | solution.py:273
  4.8 12.5 %collective-permute-start.6 = (bf16[32,3072]{1,0:T(8,128)(2,1)S(1)}, bf16[32,3072]{1,0:T(8,128)(2,1)S(1)}, u32[]{:S(2)}, u32[]{:S(2)}) collective-permute-start(bf16[32,3072]{1,0:T(8,128)(2,1)S(1)} %get-tuple-element.75), channel_id=1, source_target_pairs={{0,2},{1,3},{2,0},{3,1},{4,6},{5,7},{6,4},{7,5},{8,10},{9,11},{10,... | collective-permute-start | bytes 589832 | tf_op jit(solution)/shard_map/ppermute | solution.py:273
  10.6 7.0 %collective-permute-start.8 = (bf16[32,3072]{1,0:T(8,128)(2,1)S(1)}, bf16[32,3072]{1,0:T(8,128)(2,1)S(1)}, u32[]{:S(2)}, u32[]{:S(2)}) collective-permute-start(bf16[32,3072]{1,0:T(8,128)(2,1)S(1)} %collective-permute-done.5.refs_2_), channel_id=1, source_target_pairs={{0,8},{4,12},{8,0},{12,4},{16,24},{20,28},{24,16},{28,20},{1,9},{5... | collective-permute-start | bytes 589832 | tf_op jit(solution)/shard_map/ppermute | solution.py:273
  12.6 5.7 %collective-permute-start.7 = (bf16[32,3072]{1,0:T(8,128)(2,1)S(1)}, bf16[32,3072]{1,0:T(8,128)(2,1)S(1)}, u32[]{:S(2)}, u32[]{:S(2)}) collective-permute-start(bf16[32,3072]{1,0:T(8,128)(2,1)S(1)} %collective-permute-done.5.refs_2_), channel_id=1, source_target_pairs={{0,4},{4,0},{8,12},{12,8},{16,20},{20,16},{24,28},{28,24},{1,5},{5... | collective-permute-start | bytes 589832 | tf_op jit(solution)/shard_map/ppermute | solution.py:273
  14.1 7.9 %copy-start.2 = (bf16[128,3072]{1,0:T(8,128)(2,1)}, bf16[128,3072]{1,0:T(8,128)(2,1)S(1)}, u32[]{:S(2)}) copy-start(bf16[128,3072]{1,0:T(8,128)(2,1)S(1)} %collective-permute-done.refs_1_) | copy-start | bytes 2359300
  15.6 4.2 %collective-permute-start.1 = (f32[2,2,128]{2,0,1:T(2,128)S(1)}, f32[2,2,128]{2,0,1:T(2,128)S(1)}, u32[]{:S(2)}, u32[]{:S(2)}) collective-permute-start(f32[2,2,128]{2,0,1:T(2,128)S(1)} %get-tuple-element.153), channel_id=1, source_target_pairs={{0,1},{1,0},{2,3},{3,2},{4,5},{5,4},{6,7},{7,6},{8,9},{9,8},{10,11... | collective-permute-start | bytes 6152 | tf_op jit(solution)/shard_map/ppermute | solution.py:273
  15.7 4.1 %collective-permute-start.2 = (f32[2,2,128]{2,0,1:T(2,128)S(1)}, f32[2,2,128]{2,0,1:T(2,128)S(1)}, u32[]{:S(2)}, u32[]{:S(2)}) collective-permute-start(f32[2,2,128]{2,0,1:T(2,128)S(1)} %get-tuple-element.154), channel_id=1, source_target_pairs={{0,2},{1,3},{2,0},{3,1},{4,6},{5,7},{6,4},{7,5},{8,10},{9,11},{10,... | collective-permute-start | bytes 6152 | tf_op jit(solution)/shard_map/ppermute | solution.py:273
  17.3 3.1 %collective-permute-start.3 = (f32[2,2,128]{2,0,1:T(2,128)S(1)}, f32[2,2,128]{2,0,1:T(2,128)S(1)}, u32[]{:S(2)}, u32[]{:S(2)}) collective-permute-start(f32[2,2,128]{2,0,1:T(2,128)S(1)} %get-tuple-element.155), channel_id=1, source_target_pairs={{0,3},{1,2},{2,1},{3,0},{4,7},{5,6},{6,5},{7,4},{8,11},{9,10},{10,... | collective-permute-start | bytes 6152 | tf_op jit(solution)/shard_map/ppermute | solution.py:273
  17.6 4.4 %collective-permute-start.10 = (bf16[32,3072]{1,0:T(8,128)(2,1)S(1)}, bf16[32,3072]{1,0:T(8,128)(2,1)S(1)}, u32[]{:S(2)}, u32[]{:S(2)}) collective-permute-start(bf16[32,3072]{1,0:T(8,128)(2,1)S(1)} %collective-permute-done.6.refs_3_), channel_id=1, source_target_pairs={{0,1},{1,0},{2,3},{3,2},{4,5},{5,4},{6,7},{7,6},{8,9},{9,8},{10,11... | collective-permute-start | bytes 589832 | tf_op jit(solution)/shard_map/ppermute | solution.py:273
  18.3 19.6 %collective-permute-start.13 = (bf16[128,3072]{1,0:T(8,128)(2,1)}, bf16[128,3072]{1,0:T(8,128)(2,1)S(1)}, u32[]{:S(2)}, u32[]{:S(2)}) collective-permute-start(bf16[128,3072]{1,0:T(8,128)(2,1)} %refs_0_.1), channel_id=1, source_target_pairs={{0,2},{1,3},{2,0},{3,1},{4,6},{5,7},{6,4},{7,5},{8,10},{9,11},{10,... | collective-permute-start | bytes 2359304 | tf_op jit(solution)/shard_map/ppermute | solution.py:273
  19.9 1.7 %collective-permute-start.9 = (bf16[32,3072]{1,0:T(8,128)(2,1)S(1)}, bf16[32,3072]{1,0:T(8,128)(2,1)S(1)}, u32[]{:S(2)}, u32[]{:S(2)}) collective-permute-start(bf16[32,3072]{1,0:T(8,128)(2,1)S(1)} %collective-permute-done.5.refs_2_), channel_id=1, source_target_pairs={{0,1},{1,0},{2,3},{3,2},{4,5},{5,4},{6,7},{7,6},{8,9},{9,8},{10,11... | collective-permute-start | bytes 589832 | tf_op jit(solution)/shard_map/ppermute | solution.py:273
  19.9 2.1 %collective-permute-start.12 = (bf16[32,3072]{1,0:T(8,128)(2,1)S(1)}, bf16[32,3072]{1,0:T(8,128)(2,1)S(1)}, u32[]{:S(2)}, u32[]{:S(2)}) collective-permute-start(bf16[32,3072]{1,0:T(8,128)(2,1)S(1)} %collective-permute-done.8.refs_5_), channel_id=1, source_target_pairs={{0,1},{1,0},{2,3},{3,2},{4,5},{5,4},{6,7},{7,6},{8,9},{9,8},{10,11... | collective-permute-start | bytes 589832 | tf_op jit(solution)/shard_map/ppermute | solution.py:273
  20.4 1.6 %collective-permute-start.11 = (bf16[32,3072]{1,0:T(8,128)(2,1)S(1)}, bf16[32,3072]{1,0:T(8,128)(2,1)S(1)}, u32[]{:S(2)}, u32[]{:S(2)}) collective-permute-start(bf16[32,3072]{1,0:T(8,128)(2,1)S(1)} %collective-permute-done.7.refs_4_), channel_id=1, source_target_pairs={{0,1},{1,0},{2,3},{3,2},{4,5},{5,4},{6,7},{7,6},{8,9},{9,8},{10,11... | collective-permute-start | bytes 589832 | tf_op jit(solution)/shard_map/ppermute | solution.py:273
  21.5 18.8 %copy-start.1 = (bf16[128,3072]{1,0:T(8,128)(2,1)S(1)}, bf16[128,3072]{1,0:T(8,128)(2,1)}, u32[]{:S(2)}) copy-start(bf16[128,3072]{1,0:T(8,128)(2,1)} %refs_0_.1) | copy-start | bytes 2359300
  21.5 16.6 %collective-permute-start.4 = (bf16[128,3072]{1,0:T(8,128)(2,1)}, bf16[128,3072]{1,0:T(8,128)(2,1)S(1)}, u32[]{:S(2)}, u32[]{:S(2)}) collective-permute-start(bf16[128,3072]{1,0:T(8,128)(2,1)} %refs_0_.1), channel_id=1, source_target_pairs={{0,1},{1,0},{2,3},{3,2},{4,5},{5,4},{6,7},{7,6},{8,9},{9,8},{10,11... | collective-permute-start | bytes 2359304 | tf_op jit(solution)/shard_map/ppermute | solution.py:273
  38.0 2.4 %collective-permute-start.14 = (bf16[128,3072]{1,0:T(8,128)(2,1)S(1)}, bf16[128,3072]{1,0:T(8,128)(2,1)S(1)}, u32[]{:S(2)}, u32[]{:S(2)}) collective-permute-start(bf16[128,3072]{1,0:T(8,128)(2,1)S(1)} %collective-permute-done.13.refs_2_), channel_id=1, source_target_pairs={{0,1},{1,0},{2,3},{3,2},{4,5},{5,4},{6,7},{7,6},{8,9},{9,8},{10,11... | collective-permute-start | bytes 2359304 | tf_op jit(solution)/shard_map/ppermute | solution.py:273
  58.3 8.8 %collective-permute-start.16 = (bf16[256,1536]{1,0:T(8,128)(2,1)S(1)}, bf16[256,1536]{1,0:T(8,128)(2,1)S(1)}, u32[]{:S(2)}, u32[]{:S(2)}) collective-permute-start(bf16[256,1536]{1,0:T(8,128)(2,1)S(1)} %get-tuple-element.88), channel_id=1, source_target_pairs={{0,1},{1,0},{2,3},{3,2},{4,5},{5,4},{6,7},{7,6},{8,9},{9,8},{10,11... | collective-permute-start | bytes 2359304 | tf_op jit(solution)/shard_map/ppermute | solution.py:273
  66.6 2.4 %collective-permute-start.15 = (bf16[256,1536]{1,0:T(8,128)(2,1)S(1)}, bf16[256,1536]{1,0:T(8,128)(2,1)S(1)}, u32[]{:S(2)}, u32[]{:S(2)}) collective-permute-start(bf16[256,1536]{1,0:T(8,128)(2,1)S(1)} %get-tuple-element.86), channel_id=1, source_target_pairs={{0,1},{1,0},{2,3},{3,2},{4,5},{5,4},{6,7},{7,6},{8,9},{9,8},{10,11... | collective-permute-start | bytes 2359304 | tf_op jit(solution)/shard_map/ppermute | solution.py:273
  67.1 7.0 %copy-start = (bf16[2,320,3072]{2,1,0:T(8,128)(2,1)S(1)}, bf16[2,320,3072]{2,1,0:T(8,128)(2,1)}, u32[]{:S(2)}) copy-start(bf16[2,320,3072]{2,1,0:T(8,128)(2,1)} %get-tuple-element.123.rows) | copy-start | bytes 11796484
  69.2 13.2 %collective-permute-start.17 = (bf16[128,1536]{1,0:T(8,128)(2,1)S(1)}, bf16[128,1536]{1,0:T(8,128)(2,1)S(1)}, u32[]{:S(2)}, u32[]{:S(2)}) collective-permute-start(bf16[128,1536]{1,0:T(8,128)(2,1)S(1)} %slice.175), channel_id=1, source_target_pairs={{0,2},{1,3},{2,0},{3,1},{4,6},{5,7},{6,4},{7,5},{8,10},{9,11},{10,... | collective-permute-start | bytes 1179656 | tf_op jit(solution)/shard_map/ppermute | solution.py:273
  70.6 9.0 %collective-permute-start.18 = (bf16[64,1536]{1,0:T(8,128)(2,1)S(1)}, bf16[64,1536]{1,0:T(8,128)(2,1)S(1)}, u32[]{:S(2)}, u32[]{:S(2)}) collective-permute-start(bf16[64,1536]{1,0:T(8,128)(2,1)S(1)} %pad_maximum_fusion.1), channel_id=1, source_target_pairs={{0,8},{4,12},{8,0},{12,4},{16,24},{20,28},{24,16},{28,20},{1,9},{5... | collective-permute-start | bytes 589832 | tf_op jit(solution)/shard_map/ppermute | solution.py:273
  71.6 10.8 %collective-permute-start.19 = (bf16[64,1536]{1,0:T(8,128)(2,1)S(1)}, bf16[64,1536]{1,0:T(8,128)(2,1)S(1)}, u32[]{:S(2)}, u32[]{:S(2)}) collective-permute-start(bf16[64,1536]{1,0:T(8,128)(2,1)S(1)} %pad_maximum_fusion.2), channel_id=1, source_target_pairs={{0,4},{4,0},{8,12},{12,8},{16,20},{20,16},{24,28},{28,24},{1,5},{5... | collective-permute-start | bytes 589832 | tf_op jit(solution)/shard_map/ppermute | solution.py:273
  73.1 9.3 %collective-permute-start.20 = (bf16[64,1536]{1,0:T(8,128)(2,1)S(1)}, bf16[64,1536]{1,0:T(8,128)(2,1)S(1)}, u32[]{:S(2)}, u32[]{:S(2)}) collective-permute-start(bf16[64,1536]{1,0:T(8,128)(2,1)S(1)} %pad_maximum_fusion.3), channel_id=1, source_target_pairs={{0,12},{4,8},{8,4},{12,0},{16,28},{20,24},{24,20},{28,16},{1,13},{... | collective-permute-start | bytes 589832 | tf_op jit(solution)/shard_map/ppermute | solution.py:273
  82.6 8.6 %collective-permute-start.21 = (bf16[32,1536]{1,0:T(8,128)(2,1)S(1)}, bf16[32,1536]{1,0:T(8,128)(2,1)S(1)}, u32[]{:S(2)}, u32[]{:S(2)}) collective-permute-start(bf16[32,1536]{1,0:T(8,128)(2,1)S(1)} %get-tuple-element.102), channel_id=1, source_target_pairs={{0,8},{4,12},{8,0},{12,4},{16,24},{20,28},{24,16},{28,20},{1,9},{5... | collective-permute-start | bytes 294920 | tf_op jit(solution)/shard_map/ppermute | solution.py:273
  83.8 7.4 %collective-permute-start.22 = (bf16[32,1536]{1,0:T(8,128)(2,1)S(1)}, bf16[32,1536]{1,0:T(8,128)(2,1)S(1)}, u32[]{:S(2)}, u32[]{:S(2)}) collective-permute-start(bf16[32,1536]{1,0:T(8,128)(2,1)S(1)} %get-tuple-element.103), channel_id=1, source_target_pairs={{0,4},{4,0},{8,12},{12,8},{16,20},{20,16},{24,28},{28,24},{1,5},{5... | collective-permute-start | bytes 294920 | tf_op jit(solution)/shard_map/ppermute | solution.py:273
  84.6 6.6 %collective-permute-start.23 = (bf16[32,1536]{1,0:T(8,128)(2,1)S(1)}, bf16[32,1536]{1,0:T(8,128)(2,1)S(1)}, u32[]{:S(2)}, u32[]{:S(2)}) collective-permute-start(bf16[32,1536]{1,0:T(8,128)(2,1)S(1)} %get-tuple-element.104), channel_id=1, source_target_pairs={{0,12},{4,8},{8,4},{12,0},{16,28},{20,24},{24,20},{28,16},{1,13},{... | collective-permute-start | bytes 294920 | tf_op jit(solution)/shard_map/ppermute | solution.py:273
  86.1 5.1 %collective-permute-start.24 = (bf16[32,1536]{1,0:T(8,128)(2,1)S(1)}, bf16[32,1536]{1,0:T(8,128)(2,1)S(1)}, u32[]{:S(2)}, u32[]{:S(2)}) collective-permute-start(bf16[32,1536]{1,0:T(8,128)(2,1)S(1)} %add_convert_fusion.11), channel_id=1, source_target_pairs={{0,2},{1,3},{2,0},{3,1},{4,6},{5,7},{6,4},{7,5},{8,10},{9,11},{10,... | collective-permute-start | bytes 294920 | tf_op jit(solution)/shard_map/ppermute | solution.py:273
  91.4 10.1 %collective-permute-start.25 = (bf16[32,3072]{1,0:T(8,128)(2,1)S(1)}, bf16[32,3072]{1,0:T(8,128)(2,1)S(1)}, u32[]{:S(2)}, u32[]{:S(2)}) collective-permute-start(bf16[32,3072]{1,0:T(8,128)(2,1)S(1)} %pad_maximum_fusion.4), channel_id=1, source_target_pairs={{0,16},{4,20},{8,24},{12,28},{16,0},{20,4},{24,8},{28,12},{1,17},{... | collective-permute-start | bytes 589832 | tf_op jit(solution)/shard_map/ppermute | solution.py:273
  101.5 9.1 %collective-permute-start.28 = (bf16[32,3072]{1,0:T(8,128)(2,1)S(1)}, bf16[32,3072]{1,0:T(8,128)(2,1)S(1)}, u32[]{:S(2)}, u32[]{:S(2)}) collective-permute-start(bf16[32,3072]{1,0:T(8,128)(2,1)S(1)} %add_convert_fusion.2), channel_id=1, source_target_pairs={{0,12},{4,8},{8,4},{12,0},{16,28},{20,24},{24,20},{28,16},{1,13},{... | collective-permute-start | bytes 589832 | tf_op jit(solution)/shard_map/ppermute | solution.py:273
  102.8 9.2 %collective-permute-start.27 = (bf16[32,3072]{1,0:T(8,128)(2,1)S(1)}, bf16[32,3072]{1,0:T(8,128)(2,1)S(1)}, u32[]{:S(2)}, u32[]{:S(2)}) collective-permute-start(bf16[32,3072]{1,0:T(8,128)(2,1)S(1)} %add_convert_fusion.2), channel_id=1, source_target_pairs={{0,4},{4,0},{8,12},{12,8},{16,20},{20,16},{24,28},{28,24},{1,5},{5... | collective-permute-start | bytes 589832 | tf_op jit(solution)/shard_map/ppermute | solution.py:273
  103.3 8.7 %collective-permute-start.26 = (bf16[32,3072]{1,0:T(8,128)(2,1)S(1)}, bf16[32,3072]{1,0:T(8,128)(2,1)S(1)}, u32[]{:S(2)}, u32[]{:S(2)}) collective-permute-start(bf16[32,3072]{1,0:T(8,128)(2,1)S(1)} %add_convert_fusion.2), channel_id=1, source_target_pairs={{0,8},{4,12},{8,0},{12,4},{16,24},{20,28},{24,16},{28,20},{1,9},{5... | collective-permute-start | bytes 589832 | tf_op jit(solution)/shard_map/ppermute | solution.py:273

commit v2 on v1

--- a/solution.py
+++ b/solution.py
@@ -88,25 +88,52 @@
     ]
 
 
+def weight_tiles(step, matrices, buffers, ready):
+    _, features, tile = buffers[0].shape
+    tiles = matrices[0].shape[2] // tile
+    cols = pl.ds(pl.multiple_of(step % tiles * tile, tile), tile)
+    return [
+        pltpu.make_async_copy(
+            matrix.at[step // tiles, :, cols], buffer.at[step % 2], ready.at[step % 2, i]
+        )
+        for i, (matrix, buffer) in enumerate(zip(matrices, buffers))
+    ]
+
+
+def next_tiles(step, matrices, buffers, ready):
+    @pl.when(step + 1 < pl.num_programs(0))
+    def _():
+        for copy in weight_tiles(step + 1, matrices, buffers, ready):
+            copy.start()
+
+    for copy in weight_tiles(step, matrices, buffers, ready):
+        copy.wait()
+
+
 def forward_kernel(count, *refs):
     pieces, (slot, w_gate, w_up, rows_out, act, slope) = refs[:count], refs[count : count + 6]
-    held, chosen, rows, sent = refs[count + 6 :]
-    expert, tile = pl.program_id(0), pl.program_id(1)
+    held, chosen, rows, gates, ups, ready, sent = refs[count + 6 :]
+    step = pl.program_id(0)
+    tiles = pl.num_programs(0) // rows.shape[0]
+    fetching = ((w_gate, w_up), (gates, ups), ready)
     copy = pltpu.make_async_copy(rows, rows_out, sent)
 
-    @pl.when((expert == 0) & (tile == 0))
+    @pl.when(step == 0)
     def _():
+        for first in weight_tiles(step, *fetching):
+            first.start()
         dispatch(pieces, slot, held, chosen, rows)
         copy.start()
 
-    x = rows[expert]
-    gate = dot(x, w_gate[0])
-    up = dot(x, w_up[0])
+    next_tiles(step, *fetching)
+    x = rows[step // tiles]
+    gate = dot(x, gates[step % 2])
+    up = dot(x, ups[step % 2])
     sig = jax.nn.sigmoid(gate)
     act[0] = gate * sig
     slope[0] = up * sig * (1.0 + gate * (1.0 - sig))
 
-    @pl.when((expert == pl.num_programs(0) - 1) & (tile == pl.num_programs(1) - 1))
+    @pl.when(step == pl.num_programs(0) - 1)
     def _():
         copy.wait()
 
@@ -115,13 +142,15 @@
     experts, blocks, tokens = slot.shape
     _, features, units = w_gate.shape
     tile = min(UNIT_TILE, units)
+    tiles = units // tile
     slots = blocks * MOST
-    matrix = pl.BlockSpec((1, features, tile), lambda l, f: (l, 0, f))
-    unit = pl.BlockSpec((1, slots, tile), lambda l, f: (l, 0, f))
+    unit = pl.BlockSpec((1, slots, tile), lambda i: (i // tiles, 0, i % tiles))
     return pl.pallas_call(
         functools.partial(forward_kernel, len(pieces)),
-        grid=(experts, units // tile),
-        in_specs=[whole(p.shape) for p in pieces] + [whole(slot.shape), matrix, matrix],
+        grid=(experts * tiles,),
+        in_specs=[whole(p.shape) for p in pieces]
+        + [whole(slot.shape)]
+        + [pl.BlockSpec(memory_space=pl.ANY)] * 2,
         out_specs=[pl.BlockSpec(memory_space=pltpu.HBM), unit, unit],
         out_shape=[
             jax.ShapeDtypeStruct((experts, slots, features), BF16),
@@ -129,8 +158,9 @@
             jax.ShapeDtypeStruct((experts, slots, units), F32),
         ],
         scratch_shapes=dispatch_scratch(experts, blocks, tokens, features)
-        + [pltpu.SemaphoreType.DMA],
-        compiler_params=params(2, 52),
+        + [pltpu.VMEM((2, features, tile), BF16)] * 2
+        + [pltpu.SemaphoreType.DMA((2, 2)), pltpu.SemaphoreType.DMA],
+        compiler_params=params(1, 52),
         cost_estimate=pl.CostEstimate(
             flops=4 * experts * slots * features * units,
             bytes_accessed=4 * experts * features * units,
@@ -141,14 +171,19 @@
 
 def hidden_kernel(count, *refs):
     pieces, (slot, weight, act, slope, w_down) = refs[:count], refs[count : count + 5]
-    gate_grad, up_grad, held, chosen, grads = refs[count + 5 :]
-    expert = pl.program_id(0)
-
-    @pl.when((expert == 0) & (pl.program_id(1) == 0))
+    gate_grad, up_grad, held, chosen, grads, downs, ready = refs[count + 5 :]
+    step = pl.program_id(0)
+    tiles = pl.num_programs(0) // grads.shape[0]
+    fetching = ((w_down,), (downs,), ready)
+
+    @pl.when(step == 0)
     def _():
+        for first in weight_tiles(step, *fetching):
+            first.start()
         dispatch(pieces, slot, held, chosen, grads, weight)
 
-    hidden = dot(grads[expert], w_down[0])
+    next_tiles(step, *fetching)
+    hidden = dot(grads[step // tiles], downs[step % 2])
     up_grad[0] = (hidden * act[0]).astype(BF16)
     gate_grad[0] = (hidden * slope[0]).astype(BF16)
 
@@ -157,18 +192,19 @@
     experts, blocks, tokens = slot.shape
     _, features, units = w_down.shape
     tile = min(UNIT_TILE, units)
+    tiles = units // tile
     slots = blocks * MOST
-    unit = pl.BlockSpec((1, slots, tile), lambda l, f: (l, 0, f))
+    unit = pl.BlockSpec((1, slots, tile), lambda i: (i // tiles, 0, i % tiles))
     return pl.pallas_call(
         functools.partial(hidden_kernel, len(pieces)),
-        grid=(experts, units // tile),
+        grid=(experts * tiles,),
         in_specs=[whole(p.shape) for p in pieces]
-        + [whole(slot.shape), whole(slot.shape), unit, unit]
-        + [pl.BlockSpec((1, features, tile), lambda l, f: (l, 0, f))],
+        + [whole(slot.shape), whole(slot.shape), unit, unit, pl.BlockSpec(memory_space=pl.ANY)],
         out_specs=[unit, unit],
         out_shape=[jax.ShapeDtypeStruct((experts, slots, units), BF16)] * 2,
-        scratch_shapes=dispatch_scratch(experts, blocks, tokens, features),
-        compiler_params=params(2, 48),
+        scratch_shapes=dispatch_scratch(experts, blocks, tokens, features)
+        + [pltpu.VMEM((2, features, tile), BF16), pltpu.SemaphoreType.DMA((2, 1))],
+        compiler_params=params(1, 48),
         cost_estimate=pl.CostEstimate(
             flops=2 * experts * slots * features * units,
             bytes_accessed=2 * experts * features * units,
@@ -341,7 +377,9 @@
         return held, weight_grads(rows_now, gate_grad, up_grad, before, *which)
 
     def corners(value):
-        return [flip(v, "dp", step) for v, step in zip(value, (2, 1, 3))]
+        z, x, diagonal = value
+        x, diagonal = flip(x, "dp", 1), flip(diagonal, "dp", 3)
+        return [flip(z, "dp", 2), x, diagonal]
 
     def cut(value, count):
         return [value[i : i + quarter] for i in range(0, count * quarter, quarter)]
@@ -352,7 +390,9 @@
     far_a = chip_a[tokens:]
     away = [jnp.concatenate([chip_b[q], chip_b[4 + q]], axis=0) for q in (1, 2, 3)]
     (far_a, *away), grads = piece((far_a, *away), None, 0, 3)
-    got_a, got_b = flip(far_a, "expert", 2), corners(away)
+    got_x = flip(away[1], "dp", 1)
+    got_a = flip(far_a, "expert", 2)
+    got_b = [flip(away[2], "dp", 3), flip(away[0], "dp", 2), got_x]
     got_a, got_b, *grads = lax.optimization_barrier((got_a, got_b, *grads))
     own_a = [add(a, b) for a, b in zip(cut(chip_a, 4), cut(got_a, 4))]
     mine_b = add(chip_b[0], *(v[:quarter] for v in got_b))

time: 113 us -> 118 us (1.044)
  waiting for transfers between devices: 14.8 us -> 16.9 us
  Pallas kernels: 64 us -> 66 us
    pallas_call x1, Pallas kernels: 15.9 us -> 18.1 us  [forward(): pl.pallas_call(functools.partial(forward_kernel, len(pieces)), grid=(expe...]
    ppermute x29, waiting for transfers between devices: 14.8 us -> 16.9 us  [flip(): return lax.ppermute(value, axis, [(i, i ^ bit) for i in range(count)])]
  transfers between devices with their start and end apart: 29 -> 29, of which waited for: 7 -> 9; matrix products, arithmetic and copies ran while one was open for 2% -> 2% of each run, Pallas kernels for 41% -> 41%
where the time goes in v2:
time: 118 us; the launch traced here: 117 us
  Pallas kernels  66 us (56%)
  starting transfers between devices  28 us (24%)
  waiting for transfers between devices  16.9 us (14%)
  other arithmetic  3.85 us (3%)
  local copies, waits for them, and re-layouts  1.54 us (1%)
    ppermute x29, starting transfers between devices, flip(): return lax.ppermute(value, axis, [(i, i ^ bit) for i in range(count)])  28 us
    pallas_call x4, Pallas kernels, weight_grads(): pl.pallas_call(weights_kernel, grid=(steps,), in_specs=[pl.BlockSpec((1,...  22 us
    pallas_call x1, Pallas kernels, forward(): pl.pallas_call(functools.partial(forward_kernel, len(pieces)), grid=(expe...  18.1 us
    ppermute x29, waiting for transfers between devices, flip(): return lax.ppermute(value, axis, [(i, i ^ bit) for i in range(count)])  16.9 us
    pallas_call x2, Pallas kernels, input_sums(): pl.pallas_call(functools.partial(inputs_kernel, groups), grid=(steps,), i...  16.2 us
    pallas_call x1, Pallas kernels, hidden_grads(): pl.pallas_call(functools.partial(hidden_kernel, len(pieces)), grid=(exper...  9.63 us
  transfers between devices with their start and end apart: 29, of which 9 were waited for; matrix products, arithmetic and copies ran while one was open for 2% of the time, Pallas kernels for 41%

profile of v2, /device:TPU:0, one launch (start us, length us, event | category | flops | bytes accessed | tf_op | source)
XLA Modules:
  0.0 117.5 jit_solution(3834042720344770875)
XLA Ops:
  0.7 1.1 constant_dynamic-slice_fusion
  1.7 0.5 collective-permute-start
  2.3 2.6 %collective-permute-start.5 = (bf16[32,3072]{1,0:T(8,128)(2,1)S(1)}, bf16[32,3072]{1,0:T(8,128)(2,1)S(1)}, u32[]{:S(2)}, u32[]{:S(2)}) collective-permute-start(bf16[32,3072]{1,0:T(8,128)(2,1)S(1)} %get-tuple-element.74), channel_id=1, source_target_pairs={{0,2},{1,3},{2,0},{3,1},{4,6},{5,7},{6,4},{7,5},{8,10},{9,11},{10,... | collective-permute-start | bytes 589832 | tf_op jit(solution)/shard_map/ppermute | solution.py:309
  4.9 5.7 %collective-permute-done.5.refs_2_ = bf16[32,3072]{1,0:T(8,128)(2,1)S(1)} collective-permute-done((bf16[32,3072]{1,0:T(8,128)(2,1)S(1)}, bf16[32,3072]{1,0:T(8,128)(2,1)S(1)}, u32[]{:S(2)}, u32[]{:S(2)}) %collective-permute-start.5) | collective-permute-done | bytes 196640 | tf_op jit(solution)/shard_map/ppermute | solution.py:309
  10.6 2.0 %collective-permute-start.8 = (bf16[32,3072]{1,0:T(8,128)(2,1)S(1)}, bf16[32,3072]{1,0:T(8,128)(2,1)S(1)}, u32[]{:S(2)}, u32[]{:S(2)}) collective-permute-start(bf16[32,3072]{1,0:T(8,128)(2,1)S(1)} %collective-permute-done.5.refs_2_), channel_id=1, source_target_pairs={{0,8},{4,12},{8,0},{12,4},{16,24},{20,28},{24,16},{28,20},{1,9},{5... | collective-permute-start | bytes 589832 | tf_op jit(solution)/shard_map/ppermute | solution.py:309
  12.6 1.5 %collective-permute-start.7 = (bf16[32,3072]{1,0:T(8,128)(2,1)S(1)}, bf16[32,3072]{1,0:T(8,128)(2,1)S(1)}, u32[]{:S(2)}, u32[]{:S(2)}) collective-permute-start(bf16[32,3072]{1,0:T(8,128)(2,1)S(1)} %collective-permute-done.5.refs_2_), channel_id=1, source_target_pairs={{0,4},{4,0},{8,12},{12,8},{16,20},{20,16},{24,28},{28,24},{1,5},{5... | collective-permute-start | bytes 589832 | tf_op jit(solution)/shard_map/ppermute | solution.py:309
  14.1 0.7 fusion.1
  14.9 0.7 select_reduce_fusion
  15.7 1.6 %collective-permute-start.2 = (f32[2,2,128]{2,0,1:T(2,128)S(1)}, f32[2,2,128]{2,0,1:T(2,128)S(1)}, u32[]{:S(2)}, u32[]{:S(2)}) collective-permute-start(f32[2,2,128]{2,0,1:T(2,128)S(1)} %get-tuple-element.154), channel_id=1, source_target_pairs={{0,2},{1,3},{2,0},{3,1},{4,6},{5,7},{6,4},{7,5},{8,10},{9,11},{10,... | collective-permute-start | bytes 6152 | tf_op jit(solution)/shard_map/ppermute | solution.py:309
  17.3 0.3 collective-permute-start.3
  17.6 0.3 collective-permute-start.10
  17.9 0.4 collective-permute-done.7.refs_4_
  18.3 1.5 %collective-permute-start.13 = (bf16[128,3072]{1,0:T(8,128)(2,1)}, bf16[128,3072]{1,0:T(8,128)(2,1)S(1)}, u32[]{:S(2)}, u32[]{:S(2)}) collective-permute-start(bf16[128,3072]{1,0:T(8,128)(2,1)} %refs_0_.1), channel_id=1, source_target_pairs={{0,2},{1,3},{2,0},{3,1},{4,6},{5,7},{6,4},{7,5},{8,10},{9,11},{10,... | collective-permute-start | bytes 2359304 | tf_op jit(solution)/shard_map/ppermute | solution.py:309
  19.9 0.5 collective-permute-start.12
  21.1 0.2 iota_compare_fusion
  21.3 0.2 add_convert_fusion.1.back
  21.5 0.5 collective-permute-start.4
  22.0 18.1 %shard_map.94 = (bf16[2,320,3072]{2,1,0:T(8,128)(2,1)}, f32[2,320,1024]{2,1,0:T(8,128)}, f32[2,320,1024]{2,1,0:T(8,128)}) custom-call(bf16[128,3072]{1,0:T(8,128)(2,1)} %refs_0_, bf16[128,3072]{1,0:T(8,128)(2,1)} %copy-done.2, bf16[32,3072]{1,0:T(8,128)(2,1)S(1)} %collective-permute-done.5.refs_2_, bf16[32,3072]{1,0:T(8,128)(2,1)S(1)} %collective-permute-done.6.refs_3_, ...), custom_call_target="tpu_custom_call" | custom-call | flops 8053063680 | bytes 25165824 | tf_op jit(solution)/shard_map/pallas_call | solution.py:148
  40.2 0.2 collective-permute-start.14
  40.4 2.2 %collective-permute-done.14.refs_3_ = bf16[128,3072]{1,0:T(8,128)(2,1)S(1)} collective-permute-done((bf16[128,3072]{1,0:T(8,128)(2,1)S(1)}, bf16[128,3072]{1,0:T(8,128)(2,1)S(1)}, u32[]{:S(2)}, u32[]{:S(2)}) %collective-permute-start.14) | collective-permute-done | bytes 786464 | tf_op jit(solution)/shard_map/ppermute | solution.py:309
  42.5 9.6 %shard_map.95 = (bf16[2,320,1024]{2,1,0:T(8,128)(2,1)S(1)}, bf16[2,320,1024]{2,1,0:T(8,128)(2,1)S(1)}) custom-call(bf16[128,3072]{1,0:T(8,128)(2,1)S(1)} %copy-done.1, bf16[128,3072]{1,0:T(8,128)(2,1)S(1)} %collective-permute-done.4.refs_1_, bf16[128,3072]{1,0:T(8,128)(2,1)S(1)} %collective-permute-done.13.refs_2_, ...), custom_call_target="tpu_custom_call" | custom-call | flops 4026531840 | bytes 12582912 | tf_op jit(solution)/shard_map/pallas_call | solution.py:198
  52.2 8.1 %shard_map.97 = (bf16[256,1536]{1,0:T(8,128)(2,1)S(1)}, bf16[256,1536]{1,0:T(8,128)(2,1)S(1)}) custom-call(bf16[4,128,160]{2,1,0:T(8,128)(2,1)S(1)} %add_convert_fusion.1.back, bf16[2,320,1024]{2,1,0:T(8,128)(2,1)S(1)} %get-tuple-element.83.gate_grad, bf16[2,320,1024]{2,1,0:T(8,128)(2,1)S(1)} %get-tuple-element.84.up_grad, bf16[2,3072,1024]{2,1,0:T(8,128)(2,1)} %w_gate.3, ...), custom_call_target="tpu_custom_call" | custom-call | flops 4026531840 | bytes 12582912 | tf_op jit(solution)/shard_map/pallas_call | solution.py:235
  60.3 0.2 collective-permute-start.16
  60.5 8.1 %shard_map.96 = (bf16[256,1536]{1,0:T(8,128)(2,1)S(1)}, bf16[256,1536]{1,0:T(8,128)(2,1)S(1)}) custom-call(bf16[4,128,160]{2,1,0:T(8,128)(2,1)S(1)} %add_convert_fusion.1.back, bf16[2,320,1024]{2,1,0:T(8,128)(2,1)S(1)} %get-tuple-element.83.gate_grad, bf16[2,320,1024]{2,1,0:T(8,128)(2,1)S(1)} %get-tuple-element.84.up_grad, bf16[2,3072,1024]{2,1,0:T(8,128)(2,1)} %w_gate.3, ...), custom_call_target="tpu_custom_call" | custom-call | flops 4026531840 | bytes 12582912 | tf_op jit(solution)/shard_map/pallas_call | solution.py:235
  68.6 0.4 collective-permute-start.15
  69.1 0.2 add_convert_fusion
  69.3 1.7 %collective-permute-done.15 = bf16[256,1536]{1,0:T(8,128)(2,1)S(1)} collective-permute-done((bf16[256,1536]{1,0:T(8,128)(2,1)S(1)}, bf16[256,1536]{1,0:T(8,128)(2,1)S(1)}, u32[]{:S(2)}, u32[]{:S(2)}) %collective-permute-start.15) | collective-permute-done | bytes 786464 | tf_op jit(solution)/shard_map/ppermute | solution.py:309
  71.2 1.0 collective-permute-start.17
  72.1 1.0 collective-permute-start.18
  73.1 1.6 %collective-permute-start.19 = (bf16[64,1536]{1,0:T(8,128)(2,1)S(1)}, bf16[64,1536]{1,0:T(8,128)(2,1)S(1)}, u32[]{:S(2)}, u32[]{:S(2)}) collective-permute-start(bf16[64,1536]{1,0:T(8,128)(2,1)S(1)} %pad_maximum_fusion.1), channel_id=1, source_target_pairs={{0,8},{4,12},{8,0},{12,4},{16,24},{20,28},{24,16},{28,20},{1,9},{5... | collective-permute-start | bytes 589832 | tf_op jit(solution)/shard_map/ppermute | solution.py:309
  74.7 0.9 collective-permute-start.20
  75.6 5.5 %shard_map.98 = (f32[2,3072,1024]{2,1,0:T(8,128)}, f32[2,3072,1024]{2,1,0:T(8,128)}) custom-call(bf16[2,320,3072]{2,1,0:T(8,128)(2,1)S(1)} %copy-done, bf16[2,320,1024]{2,1,0:T(8,128)(2,1)S(1)} %get-tuple-element.83.gate_grad, bf16[2,320,1024]{2,1,0:T(8,128)(2,1)S(1)} %get-tuple-element.84.up_grad), custom_call_target="tpu_custom_call" | custom-call | flops 2013265920 | bytes 12582912 | tf_op jit(solution)/shard_map/pallas_call | solution.py:274
  81.1 2.7 %collective-permute-done.19 = bf16[64,1536]{1,0:T(8,128)(2,1)S(1)} collective-permute-done((bf16[64,1536]{1,0:T(8,128)(2,1)S(1)}, bf16[64,1536]{1,0:T(8,128)(2,1)S(1)}, u32[]{:S(2)}, u32[]{:S(2)}) %collective-permute-start.19) | collective-permute-done | bytes 196640 | tf_op jit(solution)/shard_map/ppermute | solution.py:309
  84.1 0.5 collective-permute-start.21
  84.6 1.3 %collective-permute-start.22 = (bf16[32,1536]{1,0:T(8,128)(2,1)S(1)}, bf16[32,1536]{1,0:T(8,128)(2,1)S(1)}, u32[]{:S(2)}, u32[]{:S(2)}) collective-permute-start(bf16[32,1536]{1,0:T(8,128)(2,1)S(1)} %get-tuple-element.103), channel_id=1, source_target_pairs={{0,4},{4,0},{8,12},{12,8},{16,20},{20,16},{24,28},{28,24},{1,5},{5... | collective-permute-start | bytes 294920 | tf_op jit(solution)/shard_map/ppermute | solution.py:309
  85.9 1.7 %collective-permute-start.23 = (bf16[32,1536]{1,0:T(8,128)(2,1)S(1)}, bf16[32,1536]{1,0:T(8,128)(2,1)S(1)}, u32[]{:S(2)}, u32[]{:S(2)}) collective-permute-start(bf16[32,1536]{1,0:T(8,128)(2,1)S(1)} %get-tuple-element.104), channel_id=1, source_target_pairs={{0,12},{4,8},{8,4},{12,0},{16,28},{20,24},{24,20},{28,16},{1,13},{... | collective-permute-start | bytes 294920 | tf_op jit(solution)/shard_map/ppermute | solution.py:309
  87.6 1.4 %collective-permute-start.24 = (bf16[32,1536]{1,0:T(8,128)(2,1)S(1)}, bf16[32,1536]{1,0:T(8,128)(2,1)S(1)}, u32[]{:S(2)}, u32[]{:S(2)}) collective-permute-start(bf16[32,1536]{1,0:T(8,128)(2,1)S(1)} %add_convert_fusion.11), channel_id=1, source_target_pairs={{0,2},{1,3},{2,0},{3,1},{4,6},{5,7},{6,4},{7,5},{8,10},{9,11},{10,... | collective-permute-start | bytes 294920 | tf_op jit(solution)/shard_map/ppermute | solution.py:309
  89.1 4.1 %shard_map.99 = (f32[2,3072,1024]{2,1,0:T(8,128)}, f32[2,3072,1024]{2,1,0:T(8,128)}) custom-call(bf16[2,320,3072]{2,1,0:T(8,128)(2,1)S(1)} %copy-done, bf16[2,320,1024]{2,1,0:T(8,128)(2,1)S(1)} %get-tuple-element.83.gate_grad, bf16[2,320,1024]{2,1,0:T(8,128)(2,1)S(1)} %get-tuple-element.84.up_grad, ...), custom_call_target="tpu_custom_call", output_to_operand_aliasing={{0}: (3, {}), {1}: (4, {})} | custom-call | flops 1342177280 | bytes 8388608 | tf_op jit(solution)/shard_map/pallas_call | solution.py:274
  93.4 2.7 %collective-permute-start.25 = (bf16[32,3072]{1,0:T(8,128)(2,1)S(1)}, bf16[32,3072]{1,0:T(8,128)(2,1)S(1)}, u32[]{:S(2)}, u32[]{:S(2)}) collective-permute-start(bf16[32,3072]{1,0:T(8,128)(2,1)S(1)} %pad_maximum_fusion.4), channel_id=1, source_target_pairs={{0,16},{4,20},{8,24},{12,28},{16,0},{20,4},{24,8},{28,12},{1,17},{... | collective-permute-start | bytes 589832 | tf_op jit(solution)/shard_map/ppermute | solution.py:309
  96.1 6.8 %shard_map.100 = (f32[2,3072,1024]{2,1,0:T(8,128)}, f32[2,3072,1024]{2,1,0:T(8,128)}) custom-call(bf16[2,320,3072]{2,1,0:T(8,128)(2,1)S(1)} %copy-done, bf16[2,320,1024]{2,1,0:T(8,128)(2,1)S(1)} %get-tuple-element.83.gate_grad, bf16[2,320,1024]{2,1,0:T(8,128)(2,1)S(1)} %get-tuple-element.84.up_grad, ...), custom_call_target="tpu_custom_call", output_to_operand_aliasing={{0}: (3, {}), {1}: (4, {})} | custom-call | flops 2684354560 | bytes 16777216 | tf_op jit(solution)/shard_map/pallas_call | solution.py:274
  102.9 1.2 %collective-permute-done.25 = bf16[32,3072]{1,0:T(8,128)(2,1)S(1)} collective-permute-done((bf16[32,3072]{1,0:T(8,128)(2,1)S(1)}, bf16[32,3072]{1,0:T(8,128)(2,1)S(1)}, u32[]{:S(2)}, u32[]{:S(2)}) %collective-permute-start.25) | collective-permute-done | bytes 196640 | tf_op jit(solution)/shard_map/ppermute | solution.py:309
  104.2 0.8 collective-permute-start.28
  104.9 0.9 collective-permute-start.27
  105.8 1.9 %collective-permute-start.26 = (bf16[32,3072]{1,0:T(8,128)(2,1)S(1)}, bf16[32,3072]{1,0:T(8,128)(2,1)S(1)}, u32[]{:S(2)}, u32[]{:S(2)}) collective-permute-start(bf16[32,3072]{1,0:T(8,128)(2,1)S(1)} %add_convert_fusion.2), channel_id=1, source_target_pairs={{0,8},{4,12},{8,0},{12,4},{16,24},{20,28},{24,16},{28,20},{1,9},{5... | collective-permute-start | bytes 589832 | tf_op jit(solution)/shard_map/ppermute | solution.py:309
  107.7 5.5 %shard_map.101 = (f32[2,3072,1024]{2,1,0:T(8,128)}, f32[2,3072,1024]{2,1,0:T(8,128)}) custom-call(bf16[2,320,3072]{2,1,0:T(8,128)(2,1)S(1)} %copy-done, bf16[2,320,1024]{2,1,0:T(8,128)(2,1)S(1)} %get-tuple-element.83.gate_grad, bf16[2,320,1024]{2,1,0:T(8,128)(2,1)S(1)} %get-tuple-element.84.up_grad, ...), custom_call_target="tpu_custom_call", output_to_operand_aliasing={{0}: (3, {}), {1}: (4, {})} | custom-call | flops 2013265920 | bytes 12582912 | tf_op jit(solution)/shard_map/pallas_call | solution.py:274
  113.2 2.1 %collective-permute-done.27 = bf16[32,3072]{1,0:T(8,128)(2,1)S(1)} collective-permute-done((bf16[32,3072]{1,0:T(8,128)(2,1)S(1)}, bf16[32,3072]{1,0:T(8,128)(2,1)S(1)}, u32[]{:S(2)}, u32[]{:S(2)}) %collective-permute-start.27) | collective-permute-done | bytes 196640 | tf_op jit(solution)/shard_map/ppermute | solution.py:309
  115.3 0.9 collective-permute-done.26
  116.5 1.0 reverse_select_fusion
  (63 shorter events, 1.9 us)
Async XLA Ops:
  1.7 12.4 %collective-permute-start = (bf16[128,3072]{1,0:T(8,128)(2,1)}, bf16[128,3072]{1,0:T(8,128)(2,1)S(1)}, u32[]{:S(2)}, u32[]{:S(2)}) collective-permute-start(bf16[128,3072]{1,0:T(8,128)(2,1)} %refs_0_), channel_id=1, source_target_pairs={{0,1},{1,0},{2,3},{3,2},{4,5},{5,4},{6,7},{7,6},{8,9},{9,8},{10,11... | collective-permute-start | bytes 2359304 | tf_op jit(solution)/shard_map/ppermute | solution.py:309
  2.3 8.4 %collective-permute-start.5 = (bf16[32,3072]{1,0:T(8,128)(2,1)S(1)}, bf16[32,3072]{1,0:T(8,128)(2,1)S(1)}, u32[]{:S(2)}, u32[]{:S(2)}) collective-permute-start(bf16[32,3072]{1,0:T(8,128)(2,1)S(1)} %get-tuple-element.74), channel_id=1, source_target_pairs={{0,2},{1,3},{2,0},{3,1},{4,6},{5,7},{6,4},{7,5},{8,10},{9,11},{10,... | collective-permute-start | bytes 589832 | tf_op jit(solution)/shard_map/ppermute | solution.py:309
  4.8 12.5 %collective-permute-start.6 = (bf16[32,3072]{1,0:T(8,128)(2,1)S(1)}, bf16[32,3072]{1,0:T(8,128)(2,1)S(1)}, u32[]{:S(2)}, u32[]{:S(2)}) collective-permute-start(bf16[32,3072]{1,0:T(8,128)(2,1)S(1)} %get-tuple-element.75), channel_id=1, source_target_pairs={{0,2},{1,3},{2,0},{3,1},{4,6},{5,7},{6,4},{7,5},{8,10},{9,11},{10,... | collective-permute-start | bytes 589832 | tf_op jit(solution)/shard_map/ppermute | solution.py:309
  10.6 7.0 %collective-permute-start.8 = (bf16[32,3072]{1,0:T(8,128)(2,1)S(1)}, bf16[32,3072]{1,0:T(8,128)(2,1)S(1)}, u32[]{:S(2)}, u32[]{:S(2)}) collective-permute-start(bf16[32,3072]{1,0:T(8,128)(2,1)S(1)} %collective-permute-done.5.refs_2_), channel_id=1, source_target_pairs={{0,8},{4,12},{8,0},{12,4},{16,24},{20,28},{24,16},{28,20},{1,9},{5... | collective-permute-start | bytes 589832 | tf_op jit(solution)/shard_map/ppermute | solution.py:309
  12.6 5.7 %collective-permute-start.7 = (bf16[32,3072]{1,0:T(8,128)(2,1)S(1)}, bf16[32,3072]{1,0:T(8,128)(2,1)S(1)}, u32[]{:S(2)}, u32[]{:S(2)}) collective-permute-start(bf16[32,3072]{1,0:T(8,128)(2,1)S(1)} %collective-permute-done.5.refs_2_), channel_id=1, source_target_pairs={{0,4},{4,0},{8,12},{12,8},{16,20},{20,16},{24,28},{28,24},{1,5},{5... | collective-permute-start | bytes 589832 | tf_op jit(solution)/shard_map/ppermute | solution.py:309
  14.1 7.9 %copy-start.2 = (bf16[128,3072]{1,0:T(8,128)(2,1)}, bf16[128,3072]{1,0:T(8,128)(2,1)S(1)}, u32[]{:S(2)}) copy-start(bf16[128,3072]{1,0:T(8,128)(2,1)S(1)} %collective-permute-done.refs_1_) | copy-start | bytes 2359300
  15.6 4.2 %collective-permute-start.1 = (f32[2,2,128]{2,0,1:T(2,128)S(1)}, f32[2,2,128]{2,0,1:T(2,128)S(1)}, u32[]{:S(2)}, u32[]{:S(2)}) collective-permute-start(f32[2,2,128]{2,0,1:T(2,128)S(1)} %get-tuple-element.153), channel_id=1, source_target_pairs={{0,1},{1,0},{2,3},{3,2},{4,5},{5,4},{6,7},{7,6},{8,9},{9,8},{10,11... | collective-permute-start | bytes 6152 | tf_op jit(solution)/shard_map/ppermute | solution.py:309
  15.7 4.1 %collective-permute-start.2 = (f32[2,2,128]{2,0,1:T(2,128)S(1)}, f32[2,2,128]{2,0,1:T(2,128)S(1)}, u32[]{:S(2)}, u32[]{:S(2)}) collective-permute-start(f32[2,2,128]{2,0,1:T(2,128)S(1)} %get-tuple-element.154), channel_id=1, source_target_pairs={{0,2},{1,3},{2,0},{3,1},{4,6},{5,7},{6,4},{7,5},{8,10},{9,11},{10,... | collective-permute-start | bytes 6152 | tf_op jit(solution)/shard_map/ppermute | solution.py:309
  17.3 3.1 %collective-permute-start.3 = (f32[2,2,128]{2,0,1:T(2,128)S(1)}, f32[2,2,128]{2,0,1:T(2,128)S(1)}, u32[]{:S(2)}, u32[]{:S(2)}) collective-permute-start(f32[2,2,128]{2,0,1:T(2,128)S(1)} %get-tuple-element.155), channel_id=1, source_target_pairs={{0,3},{1,2},{2,1},{3,0},{4,7},{5,6},{6,5},{7,4},{8,11},{9,10},{10,... | collective-permute-start | bytes 6152 | tf_op jit(solution)/shard_map/ppermute | solution.py:309
  17.6 4.4 %collective-permute-start.10 = (bf16[32,3072]{1,0:T(8,128)(2,1)S(1)}, bf16[32,3072]{1,0:T(8,128)(2,1)S(1)}, u32[]{:S(2)}, u32[]{:S(2)}) collective-permute-start(bf16[32,3072]{1,0:T(8,128)(2,1)S(1)} %collective-permute-done.6.refs_3_), channel_id=1, source_target_pairs={{0,1},{1,0},{2,3},{3,2},{4,5},{5,4},{6,7},{7,6},{8,9},{9,8},{10,11... | collective-permute-start | bytes 589832 | tf_op jit(solution)/shard_map/ppermute | solution.py:309
  18.3 21.8 %collective-permute-start.13 = (bf16[128,3072]{1,0:T(8,128)(2,1)}, bf16[128,3072]{1,0:T(8,128)(2,1)S(1)}, u32[]{:S(2)}, u32[]{:S(2)}) collective-permute-start(bf16[128,3072]{1,0:T(8,128)(2,1)} %refs_0_.1), channel_id=1, source_target_pairs={{0,2},{1,3},{2,0},{3,1},{4,6},{5,7},{6,4},{7,5},{8,10},{9,11},{10,... | collective-permute-start | bytes 2359304 | tf_op jit(solution)/shard_map/ppermute | solution.py:309
  19.9 1.7 %collective-permute-start.9 = (bf16[32,3072]{1,0:T(8,128)(2,1)S(1)}, bf16[32,3072]{1,0:T(8,128)(2,1)S(1)}, u32[]{:S(2)}, u32[]{:S(2)}) collective-permute-start(bf16[32,3072]{1,0:T(8,128)(2,1)S(1)} %collective-permute-done.5.refs_2_), channel_id=1, source_target_pairs={{0,1},{1,0},{2,3},{3,2},{4,5},{5,4},{6,7},{7,6},{8,9},{9,8},{10,11... | collective-permute-start | bytes 589832 | tf_op jit(solution)/shard_map/ppermute | solution.py:309
  19.9 2.1 %collective-permute-start.12 = (bf16[32,3072]{1,0:T(8,128)(2,1)S(1)}, bf16[32,3072]{1,0:T(8,128)(2,1)S(1)}, u32[]{:S(2)}, u32[]{:S(2)}) collective-permute-start(bf16[32,3072]{1,0:T(8,128)(2,1)S(1)} %collective-permute-done.8.refs_5_), channel_id=1, source_target_pairs={{0,1},{1,0},{2,3},{3,2},{4,5},{5,4},{6,7},{7,6},{8,9},{9,8},{10,11... | collective-permute-start | bytes 589832 | tf_op jit(solution)/shard_map/ppermute | solution.py:309
  20.4 1.6 %collective-permute-start.11 = (bf16[32,3072]{1,0:T(8,128)(2,1)S(1)}, bf16[32,3072]{1,0:T(8,128)(2,1)S(1)}, u32[]{:S(2)}, u32[]{:S(2)}) collective-permute-start(bf16[32,3072]{1,0:T(8,128)(2,1)S(1)} %collective-permute-done.7.refs_4_), channel_id=1, source_target_pairs={{0,1},{1,0},{2,3},{3,2},{4,5},{5,4},{6,7},{7,6},{8,9},{9,8},{10,11... | collective-permute-start | bytes 589832 | tf_op jit(solution)/shard_map/ppermute | solution.py:309
  21.5 21.0 %copy-start.1 = (bf16[128,3072]{1,0:T(8,128)(2,1)S(1)}, bf16[128,3072]{1,0:T(8,128)(2,1)}, u32[]{:S(2)}) copy-start(bf16[128,3072]{1,0:T(8,128)(2,1)} %refs_0_.1) | copy-start | bytes 2359300
  21.5 18.8 %collective-permute-start.4 = (bf16[128,3072]{1,0:T(8,128)(2,1)}, bf16[128,3072]{1,0:T(8,128)(2,1)S(1)}, u32[]{:S(2)}, u32[]{:S(2)}) collective-permute-start(bf16[128,3072]{1,0:T(8,128)(2,1)} %refs_0_.1), channel_id=1, source_target_pairs={{0,1},{1,0},{2,3},{3,2},{4,5},{5,4},{6,7},{7,6},{8,9},{9,8},{10,11... | collective-permute-start | bytes 2359304 | tf_op jit(solution)/shard_map/ppermute | solution.py:309
  40.2 2.4 %collective-permute-start.14 = (bf16[128,3072]{1,0:T(8,128)(2,1)S(1)}, bf16[128,3072]{1,0:T(8,128)(2,1)S(1)}, u32[]{:S(2)}, u32[]{:S(2)}) collective-permute-start(bf16[128,3072]{1,0:T(8,128)(2,1)S(1)} %collective-permute-done.13.refs_2_), channel_id=1, source_target_pairs={{0,1},{1,0},{2,3},{3,2},{4,5},{5,4},{6,7},{7,6},{8,9},{9,8},{10,11... | collective-permute-start | bytes 2359304 | tf_op jit(solution)/shard_map/ppermute | solution.py:309
  60.3 8.8 %collective-permute-start.16 = (bf16[256,1536]{1,0:T(8,128)(2,1)S(1)}, bf16[256,1536]{1,0:T(8,128)(2,1)S(1)}, u32[]{:S(2)}, u32[]{:S(2)}) collective-permute-start(bf16[256,1536]{1,0:T(8,128)(2,1)S(1)} %get-tuple-element.88), channel_id=1, source_target_pairs={{0,1},{1,0},{2,3},{3,2},{4,5},{5,4},{6,7},{7,6},{8,9},{9,8},{10,11... | collective-permute-start | bytes 2359304 | tf_op jit(solution)/shard_map/ppermute | solution.py:309
  68.6 2.4 %collective-permute-start.15 = (bf16[256,1536]{1,0:T(8,128)(2,1)S(1)}, bf16[256,1536]{1,0:T(8,128)(2,1)S(1)}, u32[]{:S(2)}, u32[]{:S(2)}) collective-permute-start(bf16[256,1536]{1,0:T(8,128)(2,1)S(1)} %get-tuple-element.86), channel_id=1, source_target_pairs={{0,1},{1,0},{2,3},{3,2},{4,5},{5,4},{6,7},{7,6},{8,9},{9,8},{10,11... | collective-permute-start | bytes 2359304 | tf_op jit(solution)/shard_map/ppermute | solution.py:309
  69.1 6.6 %copy-start = (bf16[2,320,3072]{2,1,0:T(8,128)(2,1)S(1)}, bf16[2,320,3072]{2,1,0:T(8,128)(2,1)}, u32[]{:S(2)}) copy-start(bf16[2,320,3072]{2,1,0:T(8,128)(2,1)} %get-tuple-element.123.rows) | copy-start | bytes 11796484
  71.2 12.7 %collective-permute-start.17 = (bf16[128,1536]{1,0:T(8,128)(2,1)S(1)}, bf16[128,1536]{1,0:T(8,128)(2,1)S(1)}, u32[]{:S(2)}, u32[]{:S(2)}) collective-permute-start(bf16[128,1536]{1,0:T(8,128)(2,1)S(1)} %slice.175), channel_id=1, source_target_pairs={{0,2},{1,3},{2,0},{3,1},{4,6},{5,7},{6,4},{7,5},{8,10},{9,11},{10,... | collective-permute-start | bytes 1179656 | tf_op jit(solution)/shard_map/ppermute | solution.py:309
  72.1 9.0 %collective-permute-start.18 = (bf16[64,1536]{1,0:T(8,128)(2,1)S(1)}, bf16[64,1536]{1,0:T(8,128)(2,1)S(1)}, u32[]{:S(2)}, u32[]{:S(2)}) collective-permute-start(bf16[64,1536]{1,0:T(8,128)(2,1)S(1)} %pad_maximum_fusion.3), channel_id=1, source_target_pairs={{0,12},{4,8},{8,4},{12,0},{16,28},{20,24},{24,20},{28,16},{1,13},{... | collective-permute-start | bytes 589832 | tf_op jit(solution)/shard_map/ppermute | solution.py:309
  73.1 10.7 %collective-permute-start.19 = (bf16[64,1536]{1,0:T(8,128)(2,1)S(1)}, bf16[64,1536]{1,0:T(8,128)(2,1)S(1)}, u32[]{:S(2)}, u32[]{:S(2)}) collective-permute-start(bf16[64,1536]{1,0:T(8,128)(2,1)S(1)} %pad_maximum_fusion.1), channel_id=1, source_target_pairs={{0,8},{4,12},{8,0},{12,4},{16,24},{20,28},{24,16},{28,20},{1,9},{5... | collective-permute-start | bytes 589832 | tf_op jit(solution)/shard_map/ppermute | solution.py:309
  74.7 9.2 %collective-permute-start.20 = (bf16[64,1536]{1,0:T(8,128)(2,1)S(1)}, bf16[64,1536]{1,0:T(8,128)(2,1)S(1)}, u32[]{:S(2)}, u32[]{:S(2)}) collective-permute-start(bf16[64,1536]{1,0:T(8,128)(2,1)S(1)} %pad_maximum_fusion.2), channel_id=1, source_target_pairs={{0,4},{4,0},{8,12},{12,8},{16,20},{20,16},{24,28},{28,24},{1,5},{5... | collective-permute-start | bytes 589832 | tf_op jit(solution)/shard_map/ppermute | solution.py:309
  84.1 9.1 %collective-permute-start.21 = (bf16[32,1536]{1,0:T(8,128)(2,1)S(1)}, bf16[32,1536]{1,0:T(8,128)(2,1)S(1)}, u32[]{:S(2)}, u32[]{:S(2)}) collective-permute-start(bf16[32,1536]{1,0:T(8,128)(2,1)S(1)} %get-tuple-element.102), channel_id=1, source_target_pairs={{0,8},{4,12},{8,0},{12,4},{16,24},{20,28},{24,16},{28,20},{1,9},{5... | collective-permute-start | bytes 294920 | tf_op jit(solution)/shard_map/ppermute | solution.py:309
  84.6 8.6 %collective-permute-start.22 = (bf16[32,1536]{1,0:T(8,128)(2,1)S(1)}, bf16[32,1536]{1,0:T(8,128)(2,1)S(1)}, u32[]{:S(2)}, u32[]{:S(2)}) collective-permute-start(bf16[32,1536]{1,0:T(8,128)(2,1)S(1)} %get-tuple-element.103), channel_id=1, source_target_pairs={{0,4},{4,0},{8,12},{12,8},{16,20},{20,16},{24,28},{28,24},{1,5},{5... | collective-permute-start | bytes 294920 | tf_op jit(solution)/shard_map/ppermute | solution.py:309
  85.9 7.3 %collective-permute-start.23 = (bf16[32,1536]{1,0:T(8,128)(2,1)S(1)}, bf16[32,1536]{1,0:T(8,128)(2,1)S(1)}, u32[]{:S(2)}, u32[]{:S(2)}) collective-permute-start(bf16[32,1536]{1,0:T(8,128)(2,1)S(1)} %get-tuple-element.104), channel_id=1, source_target_pairs={{0,12},{4,8},{8,4},{12,0},{16,28},{20,24},{24,20},{28,16},{1,13},{... | collective-permute-start | bytes 294920 | tf_op jit(solution)/shard_map/ppermute | solution.py:309
  87.6 5.6 %collective-permute-start.24 = (bf16[32,1536]{1,0:T(8,128)(2,1)S(1)}, bf16[32,1536]{1,0:T(8,128)(2,1)S(1)}, u32[]{:S(2)}, u32[]{:S(2)}) collective-permute-start(bf16[32,1536]{1,0:T(8,128)(2,1)S(1)} %add_convert_fusion.11), channel_id=1, source_target_pairs={{0,2},{1,3},{2,0},{3,1},{4,6},{5,7},{6,4},{7,5},{8,10},{9,11},{10,... | collective-permute-start | bytes 294920 | tf_op jit(solution)/shard_map/ppermute | solution.py:309
  93.4 10.7 %collective-permute-start.25 = (bf16[32,3072]{1,0:T(8,128)(2,1)S(1)}, bf16[32,3072]{1,0:T(8,128)(2,1)S(1)}, u32[]{:S(2)}, u32[]{:S(2)}) collective-permute-start(bf16[32,3072]{1,0:T(8,128)(2,1)S(1)} %pad_maximum_fusion.4), channel_id=1, source_target_pairs={{0,16},{4,20},{8,24},{12,28},{16,0},{20,4},{24,8},{28,12},{1,17},{... | collective-permute-start | bytes 589832 | tf_op jit(solution)/shard_map/ppermute | solution.py:309
  104.2 9.1 %collective-permute-start.28 = (bf16[32,3072]{1,0:T(8,128)(2,1)S(1)}, bf16[32,3072]{1,0:T(8,128)(2,1)S(1)}, u32[]{:S(2)}, u32[]{:S(2)}) collective-permute-start(bf16[32,3072]{1,0:T(8,128)(2,1)S(1)} %add_convert_fusion.2), channel_id=1, source_target_pairs={{0,12},{4,8},{8,4},{12,0},{16,28},{20,24},{24,20},{28,16},{1,13},{... | collective-permute-start | bytes 589832 | tf_op jit(solution)/shard_map/ppermute | solution.py:309
  104.9 10.4 %collective-permute-start.27 = (bf16[32,3072]{1,0:T(8,128)(2,1)S(1)}, bf16[32,3072]{1,0:T(8,128)(2,1)S(1)}, u32[]{:S(2)}, u32[]{:S(2)}) collective-permute-start(bf16[32,3072]{1,0:T(8,128)(2,1)S(1)} %add_convert_fusion.2), channel_id=1, source_target_pairs={{0,4},{4,0},{8,12},{12,8},{16,20},{20,16},{24,28},{28,24},{1,5},{5... | collective-permute-start | bytes 589832 | tf_op jit(solution)/shard_map/ppermute | solution.py:309
  105.8 10.4 %collective-permute-start.26 = (bf16[32,3072]{1,0:T(8,128)(2,1)S(1)}, bf16[32,3072]{1,0:T(8,128)(2,1)S(1)}, u32[]{:S(2)}, u32[]{:S(2)}) collective-permute-start(bf16[32,3072]{1,0:T(8,128)(2,1)S(1)} %add_convert_fusion.2), channel_id=1, source_target_pairs={{0,8},{4,12},{8,0},{12,4},{16,24},{20,28},{24,16},{28,20},{1,9},{5... | collective-permute-start | bytes 589832 | tf_op jit(solution)/shard_map/ppermute | solution.py:309
